TPU v7x, 256 devices: a whole 4x4x8 slice. The times are simulated.
256 devices in a mesh: dp: 32 (over y, x, core), cluster: 8 (over z).
Axes of the slice: x: 4, y: 4, z: 8, core: 2. Of those that a mesh axis runs over, the one named last changes fastest.
Arguments:
- embeddings: bfloat16 [65536, 1024], P('dp'), as said below
- centroids: bfloat16 [8192, 1024], P('cluster'), as said below
Outputs:
- new_centroids: float32 [8192, 1024], P('cluster', 'dp')
Inputs may be any that keep to these rules, and one draw needn't show every extreme that they name: `embeddings`: every row is nonzero. `centroids`: every row is nonzero.
All inputs are finite; a program needn't handle non-finite values.
Results may differ from a plain program's by a relative error of at most 0.00045.
The roundings to bfloat16 on the way count: a program that leaves them out, or rounds other values in their place, can miss the bound.
Values sent between devices are 32-bit elements; how exact they have to be, the bound alone decides.
No kernel may reach another device: no remote copies, remote signals or barrier semaphores. Data moves between devices by JAX's collectives and lax.ppermute only.
A program may use at most 64 MiB of HBM per device.

v0:
```python
import jax
import jax.numpy as jnp
from jax import lax
from jax.sharding import PartitionSpec as P

SCALING_PASSES = 3


SOFTNESS_LEVEL = 0.025


def normalize_rows(matrix):
    values = matrix.astype(jnp.float32)
    factor = lax.rsqrt(jnp.mean(values * values, axis=1, keepdims=True) + 1e-06)
    return (values * factor * matrix.shape[1] ** (-0.5)).astype(jnp.bfloat16)


def cosine_affinity_kernel(unit_rows, unit_centroids):
    cosine_similarity = lax.dot_general(
        unit_rows, unit_centroids, (((1,), (1,)), ((), ())), preferred_element_type=jnp.float32
    )
    return jnp.exp((cosine_similarity - 1.0) / SOFTNESS_LEVEL)


def per_device(embeddings, centroids):
    unit_rows = normalize_rows(embeddings)
    unit_centroids = normalize_rows(centroids)
    local_rows = embeddings.shape[0]
    local_centroids = centroids.shape[0]
    width = embeddings.shape[1]
    data_devices = lax.axis_size("dp")
    target = local_rows * data_devices / (local_centroids * lax.axis_size("cluster"))
    stored = cosine_affinity_kernel(unit_rows, unit_centroids)

    def current_kernel():
        return stored

    row_scale = jnp.ones((local_rows,), jnp.float32)
    for repeat in range(SCALING_PASSES):
        column_part = jnp.dot(row_scale, current_kernel(), precision=lax.Precision.HIGHEST)
        column_scale = target / lax.psum(column_part, "dp")
        row_part = jnp.dot(current_kernel(), column_scale, precision=lax.Precision.HIGHEST)
        row_scale = 1.0 / lax.psum(row_part, "cluster")
    weights = (row_scale[:, None] * current_kernel()).astype(jnp.bfloat16)
    partial_value = lax.dot_general(
        weights, unit_rows, (((0,), (0,)), ((), ())), preferred_element_type=jnp.float32
    )
    shares = lax.psum_scatter(partial_value, "dp", scatter_dimension=1, tiled=True)
    squares = lax.psum(jnp.sum(shares * shares, axis=1), "dp")
    return shares * lax.rsqrt(squares / width + 1e-06)[:, None]


def solution(mesh):
    placed = (P("dp", None), P("cluster", None))
    return jax.shard_map(
        per_device, mesh=mesh, in_specs=placed, out_specs=P("cluster", "dp"), check_vma=False
    )
```

profile of v0, /device:TPU:1, one launch (start us, length us, event | category | flops | bytes accessed | tf_op | source)
XLA Modules:
  0.0 479.0 jit_solution(15015427793591661367)
XLA Ops:
  6.5 0.0 reduce-scatter.2.cloned.1.call-start
  6.5 2.1 fusion.3
  8.6 3.1 fusion
  11.7 7.9 %multiply_exponential_fusion = f32[2048,1024]{1,0:T(8,128)S(1)} fusion(bf16[1024,1024]{1,0:T(8,128)(2,1)} %param.3, f32[1024]{0:T(1024)S(1)} %add_rsqrt_fusion.2, bf16[2048,1024]{1,0:T(8,128)(2,1)} %param.2, f32[2048]{0:T(1024)S(1)} %add_rsqrt_fusion), kind=kOutput, calls=%fused_computation.6 | convolution fusion | flops 4311744512 | bytes 14692352 | tf_op jit(solution)/shard_map/dot_general | solution.py:19
  19.6 0.0 copy-start
  19.7 3.2 copy-done
  22.9 4.0 fusion.13
  26.9 65.4 %psum.49 = f32[1024]{0:T(1024)S(1)} all-reduce(f32[1024]{0:T(1024)S(1)} %bitcast.32), channel_id=1, replica_groups=mesh['dp'=32,'cluster'=8] {'dp'}, use_global_device_ids=true, to_apply=%region_2.0 | all-reduce | flops 1024 | bytes 8192 | tf_op jit(solution)/shard_map/psum | solution.py:41
  92.3 9.4 %fusion.18 = f32[1,2048]{1,0:T(1,128)S(1)} fusion(f32[2048,1024]{1,0:T(8,128)} %copy-done, f32[1024,1]{0,1:T(1,128)S(1)} %bitcast.27), kind=kOutput, calls=%fused_computation.32 | convolution fusion | flops 25165824 | bytes 8400896 | tf_op jit(solution)/shard_map/dot_general | solution.py:42
  101.7 15.0 %psum.50 = f32[2048]{0:T(1024)S(1)} all-reduce(f32[2048]{0:T(1024)S(1)} %bitcast.22), channel_id=1, replica_groups=mesh['dp'=32,'cluster'=8] {'cluster'}, use_global_device_ids=true, to_apply=%region_3.0 | all-reduce | flops 2048 | bytes 16384 | tf_op jit(solution)/shard_map/psum | solution.py:43
  116.8 6.4 %fusion.19 = f32[1,1024]{1,0:T(1,128)S(1)} fusion(f32[2048,1]{0,1:T(1,128)S(1)} %bitcast.23, f32[2048,1024]{1,0:T(8,128)} %copy-done), kind=kOutput, calls=%fused_computation.33 | convolution fusion | flops 25165824 | bytes 8400896 | tf_op jit(solution)/shard_map/dot_general | solution.py:40
  123.1 70.8 %psum.51 = f32[1024]{0:T(1024)S(1)} all-reduce(f32[1024]{0:T(1024)S(1)} %bitcast.28), channel_id=1, replica_groups=mesh['dp'=32,'cluster'=8] {'dp'}, use_global_device_ids=true, to_apply=%region_4.0 | all-reduce | flops 1024 | bytes 8192 | tf_op jit(solution)/shard_map/psum | solution.py:41
  193.9 9.4 %fusion.20 = f32[1,2048]{1,0:T(1,128)S(1)} fusion(f32[2048,1024]{1,0:T(8,128)} %copy-done, f32[1024,1]{0,1:T(1,128)S(1)} %bitcast.29), kind=kOutput, calls=%fused_computation.34 | convolution fusion | flops 25165824 | bytes 8400896 | tf_op jit(solution)/shard_map/dot_general | solution.py:42
  203.3 11.2 %psum.52 = f32[2048]{0:T(1024)S(1)} all-reduce(f32[2048]{0:T(1024)S(1)} %bitcast.24), channel_id=1, replica_groups=mesh['dp'=32,'cluster'=8] {'cluster'}, use_global_device_ids=true, to_apply=%region_5.0 | all-reduce | flops 2048 | bytes 16384 | tf_op jit(solution)/shard_map/psum | solution.py:43
  214.6 6.4 %fusion.21 = f32[1,1024]{1,0:T(1,128)S(1)} fusion(f32[2048,1]{0,1:T(1,128)S(1)} %bitcast.25, f32[2048,1024]{1,0:T(8,128)} %copy-done), kind=kOutput, calls=%fused_computation.35 | convolution fusion | flops 25165824 | bytes 8400896 | tf_op jit(solution)/shard_map/dot_general | solution.py:40
  220.9 66.0 %psum.53 = f32[1024]{0:T(1024)S(1)} all-reduce(f32[1024]{0:T(1024)S(1)} %bitcast.30), channel_id=1, replica_groups=mesh['dp'=32,'cluster'=8] {'dp'}, use_global_device_ids=true, to_apply=%region_6.0 | all-reduce | flops 1024 | bytes 8192 | tf_op jit(solution)/shard_map/psum | solution.py:41
  287.0 9.4 %fusion.22 = f32[1,2048]{1,0:T(1,128)S(1)} fusion(f32[2048,1024]{1,0:T(8,128)} %copy-done, f32[1024,1]{0,1:T(1,128)S(1)} %bitcast.31), kind=kOutput, calls=%fused_computation.36 | convolution fusion | flops 25165824 | bytes 8400896 | tf_op jit(solution)/shard_map/dot_general | solution.py:42
  296.4 13.0 %psum.54 = f32[2048]{0:T(1024)S(1)} all-reduce(f32[2048]{0:T(1024)S(1)} %bitcast.26), channel_id=1, replica_groups=mesh['dp'=32,'cluster'=8] {'cluster'}, use_global_device_ids=true, to_apply=%region_7.0 | all-reduce | flops 2048 | bytes 16384 | tf_op jit(solution)/shard_map/psum | solution.py:43
  309.4 11.4 %fusion.6 = f32[1024,1024]{0,1:T(8,128)} fusion(f32[2048,1024]{1,0:T(8,128)} %copy-done, f32[2048]{0:T(1024)S(1)} %broadcast_divide_fusion.2, bf16[2048,1024]{1,0:T(8,128)(2,1)} %param.2, f32[2048]{0:T(1024)S(1)} %add_rsqrt_fusion), kind=kOutput, calls=%fused_computation.12 | convolution fusion | flops 4307550208 | bytes 16793600 | tf_op jit(solution)/shard_map/dot_general | solution.py:45
  320.8 0.0 reduce-scatter.2.cloned.1.call-update
  320.8 84.5 %reduce-scatter.2.cloned.1.call-done = f32[1024,32]{0,1:T(8,128)} async-done(((f32[1024,1024]{0,1:T(8,128)}), f32[1024,32]{0,1:T(8,128)}) %reduce-scatter.2.cloned.1.call-update) | async-done | bytes 131088 | tf_op jit(solution)/shard_map/reduce_scatter | solution.py:48
  405.3 0.9 multiply_reduce_fusion
  406.2 64.3 %psum.55 = f32[1024]{0:T(1024)S(1)} all-reduce(f32[1024]{0:T(1024)S(1)} %multiply_reduce_fusion), channel_id=1, replica_groups=mesh['dp'=32,'cluster'=8] {'dp'}, use_global_device_ids=true, to_apply=%region_10.0 | all-reduce | flops 1024 | bytes 8192 | tf_op jit(solution)/shard_map/psum | solution.py:49
  470.6 1.6 broadcast_multiply_fusion
  (9 shorter events, 0.1 us)
Async XLA Ops:
  6.5 398.8 %reduce-scatter.2.cloned.1.call-start = ((), (), s32[]{:S(2)}) async-start(), calls=%async_computation.1 | async-start | bytes 4325376 | tf_op jit(solution)/shard_map/reduce_scatter | solution.py:48
  19.6 3.2 copy-start
Sparse Core Ops, SparseCore 0:
  320.9 84.3 reduce-scatter.1
where the time goes:
time: 479 us
  blocking collectives  306 us (64%)
  waiting for transfers between devices  84.5 us (18%)
  matrix products  64.2 us (13%)
  between operations  13.5 us (3%)
  other arithmetic  7.69 us (2%)
    psum x3, blocking collectives, per_device(): column_scale = target / lax.psum(column_part, 'dp')  202 us
    reduce_scatter x1, waiting for transfers between devices, per_device(): lax.psum_scatter(partial_value, 'dp', scatter_dimension=1, tiled=True)  84.5 us
    psum x1, blocking collectives, per_device(): squares = lax.psum(jnp.sum(shares * shares, axis=1), 'dp')  64.3 us
    psum x3, blocking collectives, per_device(): row_scale = 1.0 / lax.psum(row_part, 'cluster')  39.3 us
    dot_general x3, matrix products, per_device(): jnp.dot(current_kernel(), column_scale, precision=lax.Precision.HIGHEST)  28.1 us
    dot_general x3, matrix products, per_device(): jnp.dot(row_scale, current_kernel(), precision=lax.Precision.HIGHEST)  16.7 us
    dot_general x1, matrix products, per_device(): lax.dot_general(weights, unit_rows, (((0,), (0,)), ((), ())), preferred_e...  11.4 us
  transfers between devices with their start and end apart: 1, of which 1 were waited for; matrix products, arithmetic and copies ran while one was open for 0% of the time, Pallas kernels for 0%

commit v1 on v0

v1 whole, which is shorter than its diff:
```python
import functools

import jax
import jax.numpy as jnp
from jax import lax
from jax.experimental import pallas as pl
from jax.experimental.pallas import tpu as pltpu
from jax.sharding import Mesh
from jax.sharding import PartitionSpec as P

SCALING_PASSES = 3
SOFTNESS_LEVEL = 0.025
LOG2_E = 1.4426950408889634
EXPONENT_SLOPE = LOG2_E / SOFTNESS_LEVEL
ROWS_DP = ("y", "x", "core")
LANES = 128
SUBLANES = 8

VMEM = pl.BlockSpec(memory_space=pltpu.VMEM)
SMEM = pl.BlockSpec(memory_space=pltpu.SMEM)


def resident(array):
    return pltpu.with_memory_space_constraint(array, pltpu.VMEM)


def params(**more):
    return pltpu.CompilerParams(vmem_limit_bytes=40 * 1024 * 1024, **more)


def unit(values):
    values = values.astype(jnp.float32)
    width = values.shape[1]
    factor = lax.rsqrt(jnp.mean(values * values, axis=1, keepdims=True) + 1e-06)
    return (values * factor * width ** (-0.5)).astype(jnp.bfloat16)


def share_order(chips_y, chips_x, share):
    order = []
    for x in range(chips_x):
        for y in range(chips_y):
            order.append((chips_x * y + x) * 2)
    for y in range(chips_y):
        for x in range(chips_x):
            order.append((chips_x * y + x) * 2 + 1)
    return order


def to_lanes(partial_ref, out_ref):
    copies = out_ref.shape[0]
    rows = []
    for group in range(partial_ref.shape[0] // LANES):
        block = partial_ref[group * LANES : (group + 1) * LANES, :]
        rows.append(jnp.sum(block.T, axis=0, keepdims=True))
    total = jnp.concatenate(rows, axis=0)
    for copy in range(copies):
        out_ref[copy] = total


def prepare_kernel(order, embeddings_ref, centroids_ref, kernel_ref, unit_ref, column_ref, centroid_scratch, partial):
    step = pl.program_id(0)
    chunk = embeddings_ref.shape[0]
    share = centroids_ref.shape[0] // len(order)

    @pl.when(step == 0)
    def _():
        for place, block in enumerate(order):
            centroid_scratch[place * share : (place + 1) * share, :] = unit(
                centroids_ref[block * share : (block + 1) * share, :]
            )
        partial[...] = jnp.zeros_like(partial)

    unit_rows = unit(embeddings_ref[...])
    start = pl.multiple_of(step * chunk, chunk)
    unit_ref[pl.ds(start, chunk), :] = unit_rows
    height = 256
    for part in range(centroid_scratch.shape[0] // height):
        rows = slice(part * height, (part + 1) * height)
        cosine = lax.dot_general(
            centroid_scratch[rows, :], unit_rows, (((1,), (1,)), ((), ())), preferred_element_type=jnp.float32
        )
        affinity = jnp.exp2((cosine - 1.0) * EXPONENT_SLOPE)
        kernel_ref[rows, pl.ds(start, chunk)] = affinity
        folded = affinity[:, :LANES]
        for tile in range(1, chunk // LANES):
            folded = folded + affinity[:, tile * LANES : (tile + 1) * LANES]
        partial[rows, :] += folded

    @pl.when(step == pl.num_programs(0) - 1)
    def _():
        to_lanes(partial, column_ref)


def row_kernel(target, columns_ref, kernel_ref, row_ref, scale_scratch):
    scale = target / jnp.sum(columns_ref[...], axis=0)
    for group in range(scale.shape[0]):
        scale_scratch[group * LANES : (group + 1) * LANES, :] = jnp.broadcast_to(
            scale[group : group + 1, :], (LANES, LANES)
        ).T
    centroids, rows = kernel_ref.shape
    tiles = rows // LANES
    height = 32

    def body(step, sums):
        start = pl.multiple_of(step * height, height)
        factor = scale_scratch[pl.ds(start, height), :]
        out = []
        for tile in range(tiles):
            product = kernel_ref[pl.ds(start, height), tile * LANES : (tile + 1) * LANES] * factor
            out.append(sums[tile] + jnp.sum(product.reshape(height // SUBLANES, SUBLANES, LANES), axis=0))
        return tuple(out)

    sums = lax.fori_loop(
        0, centroids // height, body, tuple(jnp.zeros((SUBLANES, LANES), jnp.float32) for _ in range(tiles))
    )
    total = jnp.concatenate([jnp.sum(tile, axis=0, keepdims=True) for tile in sums], axis=0)
    for copy in range(row_ref.shape[0]):
        row_ref[copy] = total


def column_kernel(rows_ref, kernel_ref, column_ref, partial):
    scale = 1.0 / jnp.sum(rows_ref[...], axis=0)
    centroids, rows = kernel_ref.shape
    tiles = rows // LANES
    height = 32
    factors = [jnp.broadcast_to(scale[tile : tile + 1, :], (SUBLANES, LANES)) for tile in range(tiles)]

    def body(step, carry):
        start = pl.multiple_of(step * height, height)
        total = None
        for tile in range(tiles):
            block = kernel_ref[pl.ds(start, height), tile * LANES : (tile + 1) * LANES]
            product = block.reshape(height // SUBLANES, SUBLANES, LANES) * factors[tile][None]
            total = product if total is None else total + product
        partial[pl.ds(start, height), :] = total.reshape(height, LANES)
        return carry

    lax.fori_loop(0, centroids // height, body, 0)
    to_lanes(partial, column_ref)


def weigh(kernel_ref, scale, weight_scratch, source, place, share):
    tiles = kernel_ref.shape[1] // LANES
    for tile in range(tiles):
        lanes = slice(tile * LANES, (tile + 1) * LANES)
        weight_scratch[place * share : (place + 1) * share, lanes] = (
            kernel_ref[pl.ds(source, share), lanes] * scale[tile : tile + 1, :]
        ).astype(jnp.bfloat16)


def sums_kernel(counts, place_ref, rows_ref, kernel_ref, unit_ref, *rest):
    outs, weight_scratch = rest[:-1], rest[-1]
    slow, fast = counts
    half = slow * fast
    share = kernel_ref.shape[0] // (2 * half)
    scale = 1.0 / jnp.sum(rows_ref[...], axis=0)
    base, first, second = place_ref[0], place_ref[1], place_ref[2]
    for a in range(slow):
        for b in range(fast):
            place = a * fast + b
            block = base * half + lax.rem(first + a, slow) * fast + lax.rem(second + b, fast)
            weigh(kernel_ref, scale, weight_scratch, pl.multiple_of(block * share, share), place, share)
    height = fast * share
    if len(outs) == 1:
        outs[0][...] = jnp.dot(weight_scratch[...], unit_ref[...], preferred_element_type=jnp.float32)
    else:
        for a in range(slow):
            outs[a][...] = jnp.dot(
                weight_scratch[a * height : (a + 1) * height, :], unit_ref[...], preferred_element_type=jnp.float32
            )


def add_kernel(parts, *refs):
    received_ref = refs[0]
    kept, outs = refs[1 : 1 + parts], refs[1 + parts :]
    height = kept[0].shape[0]
    for part in range(parts):
        outs[part][...] = kept[part][...] + received_ref[part * height : (part + 1) * height, :]


def fold_kernel(parts, *refs):
    ins, outs = refs[:-parts], refs[-parts:]
    share = outs[0].shape[0]
    for part in range(parts):
        rows = slice(part * share, (part + 1) * share)
        total = ins[0][rows, :]
        for other in ins[1:]:
            total = total + other[rows, :]
        outs[part][...] = total


def finish_kernel(*refs):
    ins, out_ref, turned = refs[:-2], refs[-2], refs[-1]
    total = ins[0][...]
    for other in ins[1:]:
        total = total + other[...]
    share, width = total.shape
    factor = lax.rsqrt(jnp.mean(total * total, axis=1, keepdims=True) + 1e-06)
    total = total * factor
    repeated = jnp.concatenate([total] * (LANES // share), axis=0)
    for group in range(width // LANES):
        turned[group * LANES : (group + 1) * LANES, :] = repeated[:, group * LANES : (group + 1) * LANES].T
    slab = lax.broadcasted_iota(jnp.int32, (SUBLANES, LANES), 1) // share
    features = width // out_ref.shape[0]
    slabs = features // SUBLANES
    for owner in range(out_ref.shape[0]):
        tile = turned[owner * features : owner * features + SUBLANES, :]
        for j in range(1, slabs):
            start = owner * features + j * SUBLANES
            tile = jnp.where(slab == j, turned[start : start + SUBLANES, :], tile)
        out_ref[owner] = tile


def place_kernel(tiles_ref, out_ref):
    owners = tiles_ref.shape[0]
    centroids, features = out_ref.shape
    share = centroids // owners
    per = LANES // share
    slab = lax.broadcasted_iota(jnp.int32, (SUBLANES, LANES), 1) // share
    for group in range(owners // per):
        slabs = []
        for j in range(features // SUBLANES):
            made = None
            for s in range(per):
                tile = tiles_ref[group * per + s]
                shift = (share * (s - j)) % LANES
                moved = pltpu.roll(tile, shift, 1) if shift else tile
                made = moved if made is None else jnp.where(slab == s, moved, made)
            slabs.append(made)
        block = jnp.concatenate(slabs + [jnp.zeros((LANES - features, LANES), jnp.float32)], axis=0)
        out_ref[group * LANES : (group + 1) * LANES, :] = block.T[:, :features]


def ring(count, step):
    return [(i, (i + step) % count) for i in range(count)]


def per_device(sizes, embeddings, centroids):
    chips_y, chips_x, cores, clusters = sizes
    owners = chips_y * chips_x * cores
    rows, width = embeddings.shape
    local = centroids.shape[0]
    share = local // owners
    target = rows * owners / (local * clusters)
    order = share_order(chips_y, chips_x, share)
    f32, bf16 = jnp.float32, jnp.bfloat16
    chunk = 256

    kernel, unit_rows, columns = pl.pallas_call(
        functools.partial(prepare_kernel, order),
        grid=(rows // chunk,),
        in_specs=[
            pl.BlockSpec((chunk, width), lambda i: (i, 0)),
            pl.BlockSpec((local, width), lambda i: (0, 0)),
        ],
        out_specs=[VMEM, VMEM, VMEM],
        out_shape=[
            pltpu.VMEM((local, rows), f32),
            pltpu.VMEM((rows, width), bf16),
            pltpu.VMEM((owners, local // LANES, LANES), f32),
        ],
        scratch_shapes=[pltpu.VMEM((local, width), bf16), pltpu.VMEM((local, LANES), f32)],
        compiler_params=params(),
        name="prepare",
    )(embeddings, centroids)

    def column_exchange(sums):
        return lax.all_to_all(sums, ROWS_DP, 0, 0)

    def row_exchange(sums):
        return lax.all_to_all(sums, "cluster", 0, 0)

    for sweep in range(SCALING_PASSES):
        if sweep:
            columns = pl.pallas_call(
                column_kernel,
                in_specs=[VMEM, VMEM],
                out_specs=VMEM,
                out_shape=pltpu.VMEM((owners, local // LANES, LANES), f32),
                scratch_shapes=[pltpu.VMEM((local, LANES), f32)],
                compiler_params=params(),
                name="columns",
            )(resident(row_sums), resident(kernel))
        columns = column_exchange(columns)
        row_sums = pl.pallas_call(
            functools.partial(row_kernel, target),
            in_specs=[VMEM, VMEM],
            out_specs=VMEM,
            out_shape=pltpu.VMEM((clusters, rows // LANES, LANES), f32),
            scratch_shapes=[pltpu.VMEM((local, LANES), f32)],
            compiler_params=params(),
            name="rows",
        )(resident(columns), resident(kernel))
        row_sums = row_exchange(row_sums)

    y, x, core = (lax.axis_index(name).astype(jnp.int32) for name in ROWS_DP)
    half = owners // cores * share

    def weighted(owner_core, parts):
        first = jnp.where(owner_core == 0, x, y)
        second = jnp.where(owner_core == 0, y, x)
        place = jnp.stack([owner_core, first, second])
        return pl.pallas_call(
            functools.partial(sums_kernel, (chips_x, chips_y)),
            in_specs=[SMEM, VMEM, VMEM, VMEM],
            out_specs=[VMEM] * parts,
            out_shape=[pltpu.VMEM((half // parts, width), f32)] * parts,
            scratch_shapes=[pltpu.VMEM((half, rows), bf16)],
            compiler_params=params(),
            cost_estimate=pl.CostEstimate(
                flops=2 * half * rows * width, bytes_accessed=4 * half * (rows + width), transcendentals=0
            ),
            name="sums",
        )(place, resident(row_sums), resident(kernel), resident(unit_rows))

    (given,) = weighted(1 - core, 1)
    received = lax.ppermute(given, "core", ring(2, 1))
    kept = weighted(core, chips_x)

    first_parts = pl.pallas_call(
        functools.partial(add_kernel, chips_x),
        in_specs=[VMEM] * (1 + chips_x),
        out_specs=[VMEM] * chips_x,
        out_shape=[pltpu.VMEM((half // chips_x, width), f32)] * chips_x,
        compiler_params=params(),
        name="cores",
    )(resident(received), *[resident(part) for part in kept])

    def stage(parts, x_core):
        got = [parts[0]]
        for k in (1, 3, 2):
            pairs = []
            for j in range(chips_y):
                for i in range(chips_x):
                    for c in range(cores):
                        if c == x_core:
                            to = (j * chips_x + (i + k) % chips_x) * cores + c
                        else:
                            to = ((j + k) % chips_y * chips_x + i) * cores + c
                        pairs.append(((j * chips_x + i) * cores + c, to))
            got.append(lax.ppermute(parts[k], ROWS_DP, pairs))
        return got

    got = stage(first_parts, 0)
    second_parts = pl.pallas_call(
        functools.partial(fold_kernel, chips_y),
        in_specs=[VMEM] * len(got),
        out_specs=[VMEM] * chips_y,
        out_shape=[pltpu.VMEM((share, width), f32)] * chips_y,
        compiler_params=params(),
        name="fold",
    )(*[resident(part) for part in got])
    got = stage(second_parts, 1)
    tiles = pl.pallas_call(
        finish_kernel,
        in_specs=[VMEM] * len(got),
        out_specs=VMEM,
        out_shape=pltpu.VMEM((owners, SUBLANES, LANES), f32),
        scratch_shapes=[pltpu.VMEM((width, LANES), f32)],
        compiler_params=params(),
        name="finish",
    )(*[resident(part) for part in got])
    tiles = lax.all_to_all(tiles, ROWS_DP, 0, 0)
    return pl.pallas_call(
        place_kernel,
        in_specs=[VMEM],
        out_specs=VMEM,
        out_shape=jax.ShapeDtypeStruct((local, width // owners), f32),
        compiler_params=params(),
        name="place",
    )(resident(tiles))


def solution(mesh):
    clusters = mesh.shape["cluster"]
    sizes = (4, 4, 2, clusters)
    split = Mesh(mesh.devices.reshape(sizes), ROWS_DP + ("cluster",))
    return jax.shard_map(
        functools.partial(per_device, sizes),
        mesh=split,
        in_specs=(P(ROWS_DP, None), P("cluster", None)),
        out_specs=P("cluster", ROWS_DP),
        check_vma=False,
    )
```

time: 479 us -> 157 us (0.33)
  blocking collectives: 306 us -> 81.1 us
  matrix products: 64.2 us -> 0 us
  waiting for transfers between devices: 84.5 us -> 24.2 us
  Pallas kernels: 0 us -> 24.9 us
  between operations: 13.5 us -> 0.13 us
  local copies, waits for them, and re-layouts: 3.21 us -> 13.9 us
  starting transfers between devices: 0.01 us -> 10.7 us
  other arithmetic: 7.69 us -> 1.28 us
    psum x7 -> x0, blocking collectives: 306 us -> none  [the longest x3 202 us: per_device(): column_scale = target / lax.psum(column_part, 'dp')]
    reduce_scatter x1 -> x0, waiting for transfers between devices: 84.5 us -> none  [per_device(): lax.psum_scatter(partial_value, 'dp', scatter_dimension=1, tiled=True)]
    all_to_all x0 -> x6, blocking collectives: none -> 81.1 us  [the longest x3 41.2 us: column_exchange(): return lax.all_to_all(sums, ROWS_DP, 0, 0)]
    dot_general x8 -> x0, matrix products: 64.2 us -> none  [the longest x3 28.1 us: per_device(): jnp.dot(current_kernel(), column_scale, precision=lax.Precision.HIGHEST)]
    pallas_call x0 -> x12, Pallas kernels: none -> 24.9 us  [the longest x1 10.6 us: per_device(): pl.pallas_call(functools.partial(prepare_kernel, order), grid=(rows // ch...]
    ppermute x0 -> x7, waiting for transfers between devices: none -> 17.8 us  [the longest x6 17.8 us: stage(): got.append(lax.ppermute(parts[k], ROWS_DP, pairs))]
    unnamed x2 -> x12, local copies, waits for them, and re-layouts: 3.21 us -> 13.1 us
    ppermute x0 -> x7, starting transfers between devices: none -> 7.32 us  [the longest x6 5.69 us: stage(): got.append(lax.ppermute(parts[k], ROWS_DP, pairs))]
  transfers between devices with their start and end apart: 1 -> 8, of which waited for: 1 -> 5; matrix products, arithmetic and copies ran while one was open for 0% -> 1% of each run, Pallas kernels for 0% -> 2%
where the time goes in v1:
time: 157 us; the launch traced here: 156 us
  blocking collectives  81.1 us (52%)
  Pallas kernels  24.9 us (16%)
  waiting for transfers between devices  24.2 us (15%)
  local copies, waits for them, and re-layouts  13.9 us (9%)
  starting transfers between devices  10.7 us (7%)
    all_to_all x3, blocking collectives, column_exchange(): return lax.all_to_all(sums, ROWS_DP, 0, 0)  41.2 us
    all_to_all x2, blocking collectives, row_exchange(): return lax.all_to_all(sums, 'cluster', 0, 0)  24.7 us
    ppermute x6, waiting for transfers between devices, stage(): got.append(lax.ppermute(parts[k], ROWS_DP, pairs))  17.8 us
    all_to_all x1, blocking collectives, per_device(): tiles = lax.all_to_all(tiles, ROWS_DP, 0, 0)  15.2 us
    unnamed x12, local copies, waits for them, and re-layouts  13.1 us
    pallas_call x1, Pallas kernels, per_device(): pl.pallas_call(functools.partial(prepare_kernel, order), grid=(rows // ch...  10.6 us
    pallas_call x2, Pallas kernels, weighted(): pl.pallas_call(functools.partial(sums_kernel, (chips_x, chips_y)), in_spe...  7.36 us
    all_to_all x1, waiting for transfers between devices, row_exchange(): return lax.all_to_all(sums, 'cluster', 0, 0)  6.42 us
  transfers between devices with their start and end apart: 8, of which 5 were waited for; matrix products, arithmetic and copies ran while one was open for 1% of the time, Pallas kernels for 2%

profile of v1, /device:TPU:1, one launch (start us, length us, event | category | flops | bytes accessed | tf_op | source)
XLA Modules:
  0.0 156.3 jit_solution(1564285195345213966)
XLA Ops:
  0.0 10.6 %prepare.1 = (f32[1024,2048]{1,0:T(8,128)S(1)}, bf16[2048,1024]{1,0:T(8,128)(2,1)S(1)}, f32[32,8,128]{2,1,0:T(8,128)S(1)}) custom-call(bf16[2048,1024]{1,0:T(8,128)(2,1)} %embeddings_ref.1, bf16[1024,1024]{1,0:T(8,128)(2,1)} %centroids_ref.1), custom_call_target="tpu_custom_call" | custom-call | tf_op jit(solution)/shard_map/prepare/pallas_call | solution.py:249
  10.6 0.0 copy-start.3
  10.6 2.0 %copy-done.3 = bf16[2048,1024]{1,0:T(8,128)(2,1)} copy-done((bf16[2048,1024]{1,0:T(8,128)(2,1)}, bf16[2048,1024]{1,0:T(8,128)(2,1)S(1)}, u32[]{:S(2)}) %copy-start.3) | copy-done | bytes 4194328
  12.5 0.0 copy-start
  12.5 16.0 %all_to_all.35.columns_ref = f32[32,8,128]{2,1,0:T(8,128)S(1)} all-to-all(f32[32,8,128]{2,1,0:T(8,128)S(1)} %get-tuple-element.20), channel_id=1, replica_groups=mesh['y'=4,'x'=4,'core'=2,'cluster'=8] {'y','x','core'}, dimensions={0} | all-to-all | bytes 262144 | tf_op jit(solution)/shard_map/all_to_all | solution.py:268
  28.6 1.1 rows.3
  29.7 15.2 %all_to_all.36.rows_ref = f32[8,16,128]{2,1,0:T(8,128)S(1)} all-to-all(f32[8,16,128]{2,1,0:T(8,128)S(1)} %rows.3), channel_id=1, replica_groups=mesh['y'=4,'x'=4,'core'=2,'cluster'=8] {'cluster'}, dimensions={0} | all-to-all | bytes 131072 | tf_op jit(solution)/shard_map/all_to_all | solution.py:271
  44.9 1.1 columns.2
  45.9 12.7 %all_to_all.37.columns_ref = f32[32,8,128]{2,1,0:T(8,128)S(1)} all-to-all(f32[32,8,128]{2,1,0:T(8,128)S(1)} %columns.2), channel_id=1, replica_groups=mesh['y'=4,'x'=4,'core'=2,'cluster'=8] {'y','x','core'}, dimensions={0} | all-to-all | bytes 262144 | tf_op jit(solution)/shard_map/all_to_all | solution.py:268
  58.6 1.1 rows.4
  59.7 9.5 %all_to_all.38.rows_ref = f32[8,16,128]{2,1,0:T(8,128)S(1)} all-to-all(f32[8,16,128]{2,1,0:T(8,128)S(1)} %rows.4), channel_id=1, replica_groups=mesh['y'=4,'x'=4,'core'=2,'cluster'=8] {'cluster'}, dimensions={0} | all-to-all | bytes 131072 | tf_op jit(solution)/shard_map/all_to_all | solution.py:271
  69.2 1.1 columns.3
  70.3 12.5 %all_to_all.39.columns_ref = f32[32,8,128]{2,1,0:T(8,128)S(1)} all-to-all(f32[32,8,128]{2,1,0:T(8,128)S(1)} %columns.3), channel_id=1, replica_groups=mesh['y'=4,'x'=4,'core'=2,'cluster'=8] {'y','x','core'}, dimensions={0} | all-to-all | bytes 262144 | tf_op jit(solution)/shard_map/all_to_all | solution.py:268
  82.8 0.0 copy-done
  82.8 1.7 %rows.5 = f32[8,16,128]{2,1,0:T(8,128)} custom-call(f32[32,8,128]{2,1,0:T(8,128)S(1)} %all_to_all.39.columns_ref, f32[1024,2048]{1,0:T(8,128)S(1)} %get-tuple-element.21.kernel_ref), custom_call_target="tpu_custom_call" | custom-call | tf_op jit(solution)/shard_map/rows/pallas_call | solution.py:285
  84.6 3.4 %all-to-all-start.5 = ((f32[8,16,128]{2,1,0:T(8,128)}), f32[8,16,128]{2,1,0:T(8,128)S(1)}, u32[]{:S(2)}, u32[]{:S(2)}) async-start(f32[8,16,128]{2,1,0:T(8,128)} %rows.5), calls=%async_computation.5 | async-start | bytes 131072 | tf_op jit(solution)/shard_map/all_to_all | solution.py:271
  87.9 0.6 pad_add_fusion.place_ref
  88.6 6.4 %all-to-all-done.5.rows_ref = f32[8,16,128]{2,1,0:T(8,128)S(1)} async-done(((f32[8,16,128]{2,1,0:T(8,128)}), f32[8,16,128]{2,1,0:T(8,128)S(1)}, u32[]{:S(2)}, u32[]{:S(2)}) %all-to-all-start.5) | async-done | bytes 65568 | tf_op jit(solution)/shard_map/all_to_all | solution.py:271
  95.0 0.0 copy-start.1
  95.0 3.4 %copy-done.1 = f32[1024,2048]{1,0:T(8,128)S(1)} copy-done((f32[1024,2048]{1,0:T(8,128)S(1)}, f32[1024,2048]{1,0:T(8,128)}, u32[]{:S(2)}) %copy-start.1) | copy-done | bytes 8388632
  98.4 0.0 copy-start.4
  98.4 2.2 %copy-done.4 = bf16[2048,1024]{1,0:T(8,128)(2,1)S(1)} copy-done((bf16[2048,1024]{1,0:T(8,128)(2,1)S(1)}, bf16[2048,1024]{1,0:T(8,128)(2,1)}, u32[]{:S(2)}) %copy-start.4) | copy-done | bytes 4194328
  100.6 4.3 %sums.2 = f32[512,1024]{1,0:T(8,128)} custom-call(s32[3]{0:T(128)} %pad_add_fusion.place_ref, f32[8,16,128]{2,1,0:T(8,128)S(1)} %all-to-all-done.5.rows_ref, f32[1024,2048]{1,0:T(8,128)S(1)} %copy-done.1, bf16[2048,1024]{1,0:T(8,128)(2,1)S(1)} %copy-done.4), custom_call_target="tpu_custom_call" | custom-call | flops 2147483648 | bytes 6291456 | tf_op jit(solution)/shard_map/sums/pallas_call | solution.py:303
  104.9 1.6 %collective-permute-start = (f32[512,1024]{1,0:T(8,128)}, f32[512,1024]{1,0:T(8,128)S(1)}, u32[]{:S(2)}, u32[]{:S(2)}) collective-permute-start(f32[512,1024]{1,0:T(8,128)} %sums.2), channel_id=1, source_target_pairs={{0,8},{8,0},{1,9},{9,1},{2,10},{10,2},{3,11},{11,3},{4,12},{12,4},... | collective-permute-start | bytes 6291464 | tf_op jit(solution)/shard_map/ppermute | solution.py:317
  106.5 0.6 pad_add_fusion.1.place_ref
  107.2 0.0 copy-start.2
  107.2 3.4 %copy-done.2 = f32[1024,2048]{1,0:T(8,128)S(1)} copy-done((f32[1024,2048]{1,0:T(8,128)S(1)}, f32[1024,2048]{1,0:T(8,128)}, u32[]{:S(2)}) %copy-start.2) | copy-done | bytes 8388632
  110.6 0.0 copy-start.5
  110.6 2.2 %copy-done.5 = bf16[2048,1024]{1,0:T(8,128)(2,1)S(1)} copy-done((bf16[2048,1024]{1,0:T(8,128)(2,1)S(1)}, bf16[2048,1024]{1,0:T(8,128)(2,1)}, u32[]{:S(2)}) %copy-start.5) | copy-done | bytes 4194328
  112.8 3.0 %sums.3 = (f32[128,1024]{1,0:T(8,128)S(1)}, f32[128,1024]{1,0:T(8,128)S(1)}, f32[128,1024]{1,0:T(8,128)S(1)}, f32[128,1024]{1,0:T(8,128)S(1)}) custom-call(s32[3]{0:T(128)} %pad_add_fusion.1.place_ref, f32[8,16,128]{2,1,0:T(8,128)S(1)} %all-to-all-done.5.rows_ref, f32[1024,2048]{1,0:T(8,128)S(1)} %copy-done.2, bf16[2048,1024]{1,0:T(8,128)(2,1)S(1)} %copy-done.5), custom_call_target="tpu_custom_call" | custom-call | flops 2147483648 | bytes 6291456 | tf_op jit(solution)/shard_map/sums/pallas_call | solution.py:303
  115.8 0.0 collective-permute-done.refs_0_
  115.8 0.2 cores.1
  116.0 0.4 collective-permute-start.1
  116.4 2.4 %collective-permute-start.2 = (f32[128,1024]{1,0:T(8,128)S(1)}, f32[128,1024]{1,0:T(8,128)S(1)}, u32[]{:S(2)}, u32[]{:S(2)}) collective-permute-start(f32[128,1024]{1,0:T(8,128)S(1)} %get-tuple-element.29), channel_id=1, source_target_pairs={{0,48},{8,200},{16,0},{24,216},{32,16},{40,232},{48,32},{56,248},{... | collective-permute-start | bytes 1572872 | tf_op jit(solution)/shard_map/ppermute | solution.py:341
  118.8 0.0 collective-permute-start.3
  118.8 12.5 %collective-permute-done.1.refs_1_ = f32[128,1024]{1,0:T(8,128)S(1)} collective-permute-done((f32[128,1024]{1,0:T(8,128)S(1)}, f32[128,1024]{1,0:T(8,128)S(1)}, u32[]{:S(2)}, u32[]{:S(2)}) %collective-permute-start.1) | collective-permute-done | bytes 524320 | tf_op jit(solution)/shard_map/ppermute | solution.py:341
  131.2 0.0 collective-permute-done.2.refs_2_
  131.2 0.0 collective-permute-done.3.refs_3_
  131.2 0.1 fold.1
  131.3 0.4 collective-permute-start.4
  131.8 2.5 %collective-permute-start.5 = (f32[32,1024]{1,0:T(8,128)S(1)}, f32[32,1024]{1,0:T(8,128)S(1)}, u32[]{:S(2)}, u32[]{:S(2)}) collective-permute-start(f32[32,1024]{1,0:T(8,128)S(1)} %get-tuple-element.33), channel_id=1, source_target_pairs={{0,192},{8,56},{16,208},{24,8},{32,224},{40,24},{48,240},{56,40},{... | collective-permute-start | bytes 393224 | tf_op jit(solution)/shard_map/ppermute | solution.py:341
  134.3 0.0 collective-permute-start.6
  134.3 2.6 %collective-permute-done.4.refs_1_ = f32[32,1024]{1,0:T(8,128)S(1)} collective-permute-done((f32[32,1024]{1,0:T(8,128)S(1)}, f32[32,1024]{1,0:T(8,128)S(1)}, u32[]{:S(2)}, u32[]{:S(2)}) %collective-permute-start.4) | collective-permute-done | bytes 131104 | tf_op jit(solution)/shard_map/ppermute | solution.py:341
  136.9 0.7 collective-permute-done.5.refs_2_
  137.6 2.0 %collective-permute-done.6.refs_3_ = f32[32,1024]{1,0:T(8,128)S(1)} collective-permute-done((f32[32,1024]{1,0:T(8,128)S(1)}, f32[32,1024]{1,0:T(8,128)S(1)}, u32[]{:S(2)}, u32[]{:S(2)}) %collective-permute-start.6) | collective-permute-done | bytes 131104 | tf_op jit(solution)/shard_map/ppermute | solution.py:341
  139.6 0.3 finish.1
  139.9 15.2 %all_to_all.40.tiles_ref = f32[32,8,128]{2,1,0:T(8,128)S(1)} all-to-all(f32[32,8,128]{2,1,0:T(8,128)S(1)} %finish.1), channel_id=1, replica_groups=mesh['y'=4,'x'=4,'core'=2,'cluster'=8] {'y','x','core'}, dimensions={0} | all-to-all | bytes 262144 | tf_op jit(solution)/shard_map/all_to_all | solution.py:363
  155.1 0.3 place.1
  155.4 0.8 copy.3
Async XLA Ops:
  10.6 2.0 %copy-start.3 = (bf16[2048,1024]{1,0:T(8,128)(2,1)}, bf16[2048,1024]{1,0:T(8,128)(2,1)S(1)}, u32[]{:S(2)}) copy-start(bf16[2048,1024]{1,0:T(8,128)(2,1)S(1)} %get-tuple-element.22.unit_ref) | copy-start | bytes 12582916
  12.5 70.3 %copy-start = (f32[1024,2048]{1,0:T(8,128)}, f32[1024,2048]{1,0:T(8,128)S(1)}, u32[]{:S(2)}) copy-start(f32[1024,2048]{1,0:T(8,128)S(1)} %get-tuple-element.21.kernel_ref) | copy-start | bytes 25165828
  84.6 10.4 %all-to-all-start.5 = ((f32[8,16,128]{2,1,0:T(8,128)}), f32[8,16,128]{2,1,0:T(8,128)S(1)}, u32[]{:S(2)}, u32[]{:S(2)}) async-start(f32[8,16,128]{2,1,0:T(8,128)} %rows.5), calls=%async_computation.5 | async-start | bytes 131072 | tf_op jit(solution)/shard_map/all_to_all | solution.py:271
  95.0 3.4 %copy-start.1 = (f32[1024,2048]{1,0:T(8,128)S(1)}, f32[1024,2048]{1,0:T(8,128)}, u32[]{:S(2)}) copy-start(f32[1024,2048]{1,0:T(8,128)} %copy-done) | copy-start | bytes 25165828
  98.4 2.2 %copy-start.4 = (bf16[2048,1024]{1,0:T(8,128)(2,1)S(1)}, bf16[2048,1024]{1,0:T(8,128)(2,1)}, u32[]{:S(2)}) copy-start(bf16[2048,1024]{1,0:T(8,128)(2,1)} %copy-done.3) | copy-start | bytes 12582916
  104.9 10.9 %collective-permute-start = (f32[512,1024]{1,0:T(8,128)}, f32[512,1024]{1,0:T(8,128)S(1)}, u32[]{:S(2)}, u32[]{:S(2)}) collective-permute-start(f32[512,1024]{1,0:T(8,128)} %sums.2), channel_id=1, source_target_pairs={{0,8},{8,0},{1,9},{9,1},{2,10},{10,2},{3,11},{11,3},{4,12},{12,4},... | collective-permute-start | bytes 6291464 | tf_op jit(solution)/shard_map/ppermute | solution.py:317
  107.2 3.4 %copy-start.2 = (f32[1024,2048]{1,0:T(8,128)S(1)}, f32[1024,2048]{1,0:T(8,128)}, u32[]{:S(2)}) copy-start(f32[1024,2048]{1,0:T(8,128)} %copy-done) | copy-start | bytes 25165828
  110.6 2.2 %copy-start.5 = (bf16[2048,1024]{1,0:T(8,128)(2,1)S(1)}, bf16[2048,1024]{1,0:T(8,128)(2,1)}, u32[]{:S(2)}) copy-start(bf16[2048,1024]{1,0:T(8,128)(2,1)} %copy-done.3) | copy-start | bytes 12582916
  116.0 15.2 %collective-permute-start.1 = (f32[128,1024]{1,0:T(8,128)S(1)}, f32[128,1024]{1,0:T(8,128)S(1)}, u32[]{:S(2)}, u32[]{:S(2)}) collective-permute-start(f32[128,1024]{1,0:T(8,128)S(1)} %get-tuple-element.28), channel_id=1, source_target_pairs={{0,16},{8,72},{16,32},{24,88},{32,48},{40,104},{48,0},{56,120},{64... | collective-permute-start | bytes 1572872 | tf_op jit(solution)/shard_map/ppermute | solution.py:341
  116.4 14.8 %collective-permute-start.2 = (f32[128,1024]{1,0:T(8,128)S(1)}, f32[128,1024]{1,0:T(8,128)S(1)}, u32[]{:S(2)}, u32[]{:S(2)}) collective-permute-start(f32[128,1024]{1,0:T(8,128)S(1)} %get-tuple-element.29), channel_id=1, source_target_pairs={{0,48},{8,200},{16,0},{24,216},{32,16},{40,232},{48,32},{56,248},{... | collective-permute-start | bytes 1572872 | tf_op jit(solution)/shard_map/ppermute | solution.py:341
  118.8 12.5 %collective-permute-start.3 = (f32[128,1024]{1,0:T(8,128)S(1)}, f32[128,1024]{1,0:T(8,128)S(1)}, u32[]{:S(2)}, u32[]{:S(2)}) collective-permute-start(f32[128,1024]{1,0:T(8,128)S(1)} %get-tuple-element.30), channel_id=1, source_target_pairs={{0,32},{8,136},{16,48},{24,152},{32,0},{40,168},{48,16},{56,184},{... | collective-permute-start | bytes 1572872 | tf_op jit(solution)/shard_map/ppermute | solution.py:341
  131.3 5.6 %collective-permute-start.4 = (f32[32,1024]{1,0:T(8,128)S(1)}, f32[32,1024]{1,0:T(8,128)S(1)}, u32[]{:S(2)}, u32[]{:S(2)}) collective-permute-start(f32[32,1024]{1,0:T(8,128)S(1)} %get-tuple-element.32), channel_id=1, source_target_pairs={{0,64},{8,24},{16,80},{24,40},{32,96},{40,56},{48,112},{56,8},{64,... | collective-permute-start | bytes 393224 | tf_op jit(solution)/shard_map/ppermute | solution.py:341
  131.8 5.8 %collective-permute-start.5 = (f32[32,1024]{1,0:T(8,128)S(1)}, f32[32,1024]{1,0:T(8,128)S(1)}, u32[]{:S(2)}, u32[]{:S(2)}) collective-permute-start(f32[32,1024]{1,0:T(8,128)S(1)} %get-tuple-element.33), channel_id=1, source_target_pairs={{0,192},{8,56},{16,208},{24,8},{32,224},{40,24},{48,240},{56,40},{... | collective-permute-start | bytes 393224 | tf_op jit(solution)/shard_map/ppermute | solution.py:341
  134.3 5.3 %collective-permute-start.6 = (f32[32,1024]{1,0:T(8,128)S(1)}, f32[32,1024]{1,0:T(8,128)S(1)}, u32[]{:S(2)}, u32[]{:S(2)}) collective-permute-start(f32[32,1024]{1,0:T(8,128)S(1)} %get-tuple-element.34), channel_id=1, source_target_pairs={{0,128},{8,40},{16,144},{24,56},{32,160},{40,8},{48,176},{56,24},{... | collective-permute-start | bytes 393224 | tf_op jit(solution)/shard_map/ppermute | solution.py:341

commit v2 on v1

--- a/solution.py
+++ b/solution.py
@@ -17,15 +17,18 @@
 SUBLANES = 8
 
 VMEM = pl.BlockSpec(memory_space=pltpu.VMEM)
-SMEM = pl.BlockSpec(memory_space=pltpu.SMEM)
 
 
 def resident(array):
     return pltpu.with_memory_space_constraint(array, pltpu.VMEM)
 
 
-def params(**more):
-    return pltpu.CompilerParams(vmem_limit_bytes=40 * 1024 * 1024, **more)
+def streamed(array):
+    return pltpu.with_memory_space_constraint(array, pltpu.HBM)
+
+
+def params(mebibytes=4):
+    return pltpu.CompilerParams(vmem_limit_bytes=mebibytes * 1024 * 1024)
 
 
 def unit(values):
@@ -148,13 +151,15 @@
         ).astype(jnp.bfloat16)
 
 
-def sums_kernel(counts, place_ref, rows_ref, kernel_ref, unit_ref, *rest):
+def sums_kernel(counts, given, rows_ref, kernel_ref, unit_ref, *rest):
     outs, weight_scratch = rest[:-1], rest[-1]
     slow, fast = counts
     half = slow * fast
     share = kernel_ref.shape[0] // (2 * half)
     scale = 1.0 / jnp.sum(rows_ref[...], axis=0)
-    base, first, second = place_ref[0], place_ref[1], place_ref[2]
+    y, x, core = (lax.axis_index(name) for name in ROWS_DP)
+    base = 1 - core if given else core
+    first, second = jnp.where(base == 0, x, y), jnp.where(base == 0, y, x)
     for a in range(slow):
         for b in range(fast):
             place = a * fast + b
@@ -213,12 +218,11 @@
 
 def place_kernel(tiles_ref, out_ref):
     owners = tiles_ref.shape[0]
-    centroids, features = out_ref.shape
+    features, centroids = out_ref.shape
     share = centroids // owners
     per = LANES // share
     slab = lax.broadcasted_iota(jnp.int32, (SUBLANES, LANES), 1) // share
     for group in range(owners // per):
-        slabs = []
         for j in range(features // SUBLANES):
             made = None
             for s in range(per):
@@ -226,9 +230,7 @@
                 shift = (share * (s - j)) % LANES
                 moved = pltpu.roll(tile, shift, 1) if shift else tile
                 made = moved if made is None else jnp.where(slab == s, moved, made)
-            slabs.append(made)
-        block = jnp.concatenate(slabs + [jnp.zeros((LANES - features, LANES), jnp.float32)], axis=0)
-        out_ref[group * LANES : (group + 1) * LANES, :] = block.T[:, :features]
+            out_ref[j * SUBLANES : (j + 1) * SUBLANES, group * LANES : (group + 1) * LANES] = made
 
 
 def ring(count, step):
@@ -260,9 +262,9 @@
             pltpu.VMEM((owners, local // LANES, LANES), f32),
         ],
         scratch_shapes=[pltpu.VMEM((local, width), bf16), pltpu.VMEM((local, LANES), f32)],
-        compiler_params=params(),
+        compiler_params=params(16),
         name="prepare",
-    )(embeddings, centroids)
+    )(streamed(embeddings), streamed(centroids))
 
     def column_exchange(sums):
         return lax.all_to_all(sums, ROWS_DP, 0, 0)
@@ -293,29 +295,25 @@
         )(resident(columns), resident(kernel))
         row_sums = row_exchange(row_sums)
 
-    y, x, core = (lax.axis_index(name).astype(jnp.int32) for name in ROWS_DP)
     half = owners // cores * share
 
-    def weighted(owner_core, parts):
-        first = jnp.where(owner_core == 0, x, y)
-        second = jnp.where(owner_core == 0, y, x)
-        place = jnp.stack([owner_core, first, second])
+    def weighted(given, parts):
         return pl.pallas_call(
-            functools.partial(sums_kernel, (chips_x, chips_y)),
-            in_specs=[SMEM, VMEM, VMEM, VMEM],
+            functools.partial(sums_kernel, (chips_x, chips_y), given),
+            in_specs=[VMEM] * 3,
             out_specs=[VMEM] * parts,
             out_shape=[pltpu.VMEM((half // parts, width), f32)] * parts,
             scratch_shapes=[pltpu.VMEM((half, rows), bf16)],
-            compiler_params=params(),
+            compiler_params=params(8),
             cost_estimate=pl.CostEstimate(
                 flops=2 * half * rows * width, bytes_accessed=4 * half * (rows + width), transcendentals=0
             ),
             name="sums",
-        )(place, resident(row_sums), resident(kernel), resident(unit_rows))
-
-    (given,) = weighted(1 - core, 1)
+        )(resident(row_sums), resident(kernel), resident(unit_rows))
+
+    (given,) = weighted(True, 1)
     received = lax.ppermute(given, "core", ring(2, 1))
-    kept = weighted(core, chips_x)
+    kept = weighted(False, chips_x)
 
     first_parts = pl.pallas_call(
         functools.partial(add_kernel, chips_x),
@@ -361,14 +359,15 @@
         name="finish",
     )(*[resident(part) for part in got])
     tiles = lax.all_to_all(tiles, ROWS_DP, 0, 0)
-    return pl.pallas_call(
+    placed = pl.pallas_call(
         place_kernel,
         in_specs=[VMEM],
         out_specs=VMEM,
-        out_shape=jax.ShapeDtypeStruct((local, width // owners), f32),
+        out_shape=jax.ShapeDtypeStruct((width // owners, local), f32),
         compiler_params=params(),
         name="place",
     )(resident(tiles))
+    return placed.T
 
 
 def solution(mesh):

time: 157 us -> 140 us (0.89)
  local copies, waits for them, and re-layouts: 13.9 us -> 0 us
  blocking collectives: 81.1 us -> 91 us
  waiting for transfers between devices: 24.2 us -> 19.2 us
  starting transfers between devices: 10.7 us -> 7.24 us
  Pallas kernels: 24.9 us -> 22.1 us
    unnamed x12 -> x0, local copies, waits for them, and re-layouts: 13.1 us -> none
    all_to_all x2 -> x3, blocking collectives: 24.7 us -> 34.3 us  [row_exchange(): return lax.all_to_all(sums, 'cluster', 0, 0)]
    all_to_all x1 -> x0, waiting for transfers between devices: 6.42 us -> none  [row_exchange(): return lax.all_to_all(sums, 'cluster', 0, 0)]
    all_to_all x1 -> x0, starting transfers between devices: 3.35 us -> none  [row_exchange(): return lax.all_to_all(sums, 'cluster', 0, 0)]
    pallas_call x2, Pallas kernels: 7.36 us -> 4.69 us  [weighted(): pl.pallas_call(functools.partial(sums_kernel, (chips_x, chips_y), given),...]
  transfers between devices with their start and end apart: 8 -> 7, of which waited for: 5 -> 5; matrix products, arithmetic and copies ran while one was open for 1% -> 0% of each run, Pallas kernels for 2% -> 2%
where the time goes in v2:
time: 140 us
  blocking collectives  91 us (65%)
  Pallas kernels  22.1 us (16%)
  waiting for transfers between devices  19.2 us (14%)
  starting transfers between devices  7.24 us (5%)
    all_to_all x3, blocking collectives, column_exchange(): return lax.all_to_all(sums, ROWS_DP, 0, 0)  41.2 us
    all_to_all x3, blocking collectives, row_exchange(): return lax.all_to_all(sums, 'cluster', 0, 0)  34.3 us
    ppermute x6, waiting for transfers between devices, stage(): got.append(lax.ppermute(parts[k], ROWS_DP, pairs))  17.8 us
    all_to_all x1, blocking collectives, per_device(): tiles = lax.all_to_all(tiles, ROWS_DP, 0, 0)  15.6 us
    pallas_call x1, Pallas kernels, per_device(): pl.pallas_call(functools.partial(prepare_kernel, order), grid=(rows // ch...  10.6 us
    ppermute x6, starting transfers between devices, stage(): got.append(lax.ppermute(parts[k], ROWS_DP, pairs))  5.51 us
    pallas_call x2, Pallas kernels, weighted(): pl.pallas_call(functools.partial(sums_kernel, (chips_x, chips_y), given),...  4.69 us
    pallas_call x3, Pallas kernels, per_device(): pl.pallas_call(functools.partial(row_kernel, target), in_specs=[VMEM, VME...  3.29 us
  transfers between devices with their start and end apart: 7, of which 5 were waited for; matrix products, arithmetic and copies ran while one was open for 0% of the time, Pallas kernels for 2%

profile of v2, /device:TPU:1, one launch (start us, length us, event | category | flops | bytes accessed | tf_op | source)
XLA Modules:
  0.0 139.7 jit_solution(6849156503545927438)
XLA Ops:
  0.0 10.6 %prepare.1 = (f32[1024,2048]{1,0:T(8,128)S(1)}, bf16[2048,1024]{1,0:T(8,128)(2,1)S(1)}, f32[32,8,128]{2,1,0:T(8,128)S(1)}) custom-call(bf16[2048,1024]{1,0:T(8,128)(2,1)} %embeddings_ref.1, bf16[1024,1024]{1,0:T(8,128)(2,1)} %centroids_ref.1), custom_call_target="tpu_custom_call" | custom-call | tf_op jit(solution)/shard_map/prepare/pallas_call | solution.py:251
  10.6 16.0 %all_to_all.35.columns_ref = f32[32,8,128]{2,1,0:T(8,128)S(1)} all-to-all(f32[32,8,128]{2,1,0:T(8,128)S(1)} %get-tuple-element.20), channel_id=1, replica_groups=mesh['y'=4,'x'=4,'core'=2,'cluster'=8] {'y','x','core'}, dimensions={0} | all-to-all | bytes 262144 | tf_op jit(solution)/shard_map/all_to_all | solution.py:270
  26.6 1.1 rows.3
  27.7 15.2 %all_to_all.36.rows_ref = f32[8,16,128]{2,1,0:T(8,128)S(1)} all-to-all(f32[8,16,128]{2,1,0:T(8,128)S(1)} %rows.3), channel_id=1, replica_groups=mesh['y'=4,'x'=4,'core'=2,'cluster'=8] {'cluster'}, dimensions={0} | all-to-all | bytes 131072 | tf_op jit(solution)/shard_map/all_to_all | solution.py:273
  42.9 1.1 columns.2
  44.0 12.7 %all_to_all.37.columns_ref = f32[32,8,128]{2,1,0:T(8,128)S(1)} all-to-all(f32[32,8,128]{2,1,0:T(8,128)S(1)} %columns.2), channel_id=1, replica_groups=mesh['y'=4,'x'=4,'core'=2,'cluster'=8] {'y','x','core'}, dimensions={0} | all-to-all | bytes 262144 | tf_op jit(solution)/shard_map/all_to_all | solution.py:270
  56.7 1.1 rows.4
  57.8 9.5 %all_to_all.38.rows_ref = f32[8,16,128]{2,1,0:T(8,128)S(1)} all-to-all(f32[8,16,128]{2,1,0:T(8,128)S(1)} %rows.4), channel_id=1, replica_groups=mesh['y'=4,'x'=4,'core'=2,'cluster'=8] {'cluster'}, dimensions={0} | all-to-all | bytes 131072 | tf_op jit(solution)/shard_map/all_to_all | solution.py:273
  67.3 1.1 columns.3
  68.4 12.5 %all_to_all.39.columns_ref = f32[32,8,128]{2,1,0:T(8,128)S(1)} all-to-all(f32[32,8,128]{2,1,0:T(8,128)S(1)} %columns.3), channel_id=1, replica_groups=mesh['y'=4,'x'=4,'core'=2,'cluster'=8] {'y','x','core'}, dimensions={0} | all-to-all | bytes 262144 | tf_op jit(solution)/shard_map/all_to_all | solution.py:270
  80.9 1.1 rows.5
  82.0 9.5 %all_to_all.40.rows_ref = f32[8,16,128]{2,1,0:T(8,128)S(1)} all-to-all(f32[8,16,128]{2,1,0:T(8,128)S(1)} %rows.5), channel_id=1, replica_groups=mesh['y'=4,'x'=4,'core'=2,'cluster'=8] {'cluster'}, dimensions={0} | all-to-all | bytes 131072 | tf_op jit(solution)/shard_map/all_to_all | solution.py:273
  91.5 2.3 %sums.2 = f32[512,1024]{1,0:T(8,128)S(1)} custom-call(f32[8,16,128]{2,1,0:T(8,128)S(1)} %all_to_all.40.rows_ref, f32[1024,2048]{1,0:T(8,128)S(1)} %get-tuple-element.21.kernel_ref, bf16[2048,1024]{1,0:T(8,128)(2,1)S(1)} %get-tuple-element.22.unit_ref), custom_call_target="tpu_custom_call" | custom-call | flops 2147483648 | bytes 6291456 | tf_op jit(solution)/shard_map/sums/pallas_call | solution.py:301
  93.8 1.7 %collective-permute-start = (f32[512,1024]{1,0:T(8,128)S(1)}, f32[512,1024]{1,0:T(8,128)S(1)}, u32[]{:S(2)}, u32[]{:S(2)}) collective-permute-start(f32[512,1024]{1,0:T(8,128)S(1)} %sums.2), channel_id=1, source_target_pairs={{0,8},{8,0},{1,9},{9,1},{2,10},{10,2},{3,11},{11,3},{4,12},{12,4},... | collective-permute-start | bytes 6291464 | tf_op jit(solution)/shard_map/ppermute | solution.py:315
  95.6 2.3 %sums.3 = (f32[128,1024]{1,0:T(8,128)S(1)}, f32[128,1024]{1,0:T(8,128)S(1)}, f32[128,1024]{1,0:T(8,128)S(1)}, f32[128,1024]{1,0:T(8,128)S(1)}) custom-call(f32[8,16,128]{2,1,0:T(8,128)S(1)} %all_to_all.40.rows_ref, f32[1024,2048]{1,0:T(8,128)S(1)} %get-tuple-element.21.kernel_ref, bf16[2048,1024]{1,0:T(8,128)(2,1)S(1)} %get-tuple-element.22.unit_ref), custom_call_target="tpu_custom_call" | custom-call | flops 2147483648 | bytes 6291456 | tf_op jit(solution)/shard_map/sums/pallas_call | solution.py:301
  97.9 1.4 %collective-permute-done.refs_0_ = f32[512,1024]{1,0:T(8,128)S(1)} collective-permute-done((f32[512,1024]{1,0:T(8,128)S(1)}, f32[512,1024]{1,0:T(8,128)S(1)}, u32[]{:S(2)}, u32[]{:S(2)}) %collective-permute-start) | collective-permute-done | bytes 2097184 | tf_op jit(solution)/shard_map/ppermute | solution.py:315
  99.4 0.2 cores.1
  99.6 0.4 collective-permute-start.1
  100.0 2.4 %collective-permute-start.2 = (f32[128,1024]{1,0:T(8,128)S(1)}, f32[128,1024]{1,0:T(8,128)S(1)}, u32[]{:S(2)}, u32[]{:S(2)}) collective-permute-start(f32[128,1024]{1,0:T(8,128)S(1)} %get-tuple-element.29), channel_id=1, source_target_pairs={{0,48},{8,200},{16,0},{24,216},{32,16},{40,232},{48,32},{56,248},{... | collective-permute-start | bytes 1572872 | tf_op jit(solution)/shard_map/ppermute | solution.py:339
  102.3 0.0 collective-permute-start.3
  102.3 12.5 %collective-permute-done.1.refs_1_ = f32[128,1024]{1,0:T(8,128)S(1)} collective-permute-done((f32[128,1024]{1,0:T(8,128)S(1)}, f32[128,1024]{1,0:T(8,128)S(1)}, u32[]{:S(2)}, u32[]{:S(2)}) %collective-permute-start.1) | collective-permute-done | bytes 524320 | tf_op jit(solution)/shard_map/ppermute | solution.py:339
  114.8 0.0 collective-permute-done.2.refs_2_
  114.8 0.0 collective-permute-done.3.refs_3_
  114.8 0.1 fold.1
  114.9 0.3 collective-permute-start.4
  115.2 2.5 %collective-permute-start.5 = (f32[32,1024]{1,0:T(8,128)S(1)}, f32[32,1024]{1,0:T(8,128)S(1)}, u32[]{:S(2)}, u32[]{:S(2)}) collective-permute-start(f32[32,1024]{1,0:T(8,128)S(1)} %get-tuple-element.33), channel_id=1, source_target_pairs={{0,192},{8,56},{16,208},{24,8},{32,224},{40,24},{48,240},{56,40},{... | collective-permute-start | bytes 393224 | tf_op jit(solution)/shard_map/ppermute | solution.py:339
  117.7 0.0 collective-permute-start.6
  117.7 2.3 %collective-permute-done.4.refs_1_ = f32[32,1024]{1,0:T(8,128)S(1)} collective-permute-done((f32[32,1024]{1,0:T(8,128)S(1)}, f32[32,1024]{1,0:T(8,128)S(1)}, u32[]{:S(2)}, u32[]{:S(2)}) %collective-permute-start.4) | collective-permute-done | bytes 131104 | tf_op jit(solution)/shard_map/ppermute | solution.py:339
  120.0 1.0 collective-permute-done.5.refs_2_
  121.0 2.0 %collective-permute-done.6.refs_3_ = f32[32,1024]{1,0:T(8,128)S(1)} collective-permute-done((f32[32,1024]{1,0:T(8,128)S(1)}, f32[32,1024]{1,0:T(8,128)S(1)}, u32[]{:S(2)}, u32[]{:S(2)}) %collective-permute-start.6) | collective-permute-done | bytes 131104 | tf_op jit(solution)/shard_map/ppermute | solution.py:339
  123.0 0.3 finish.1
  123.3 15.6 %all_to_all.41.tiles_ref = f32[32,8,128]{2,1,0:T(8,128)S(1)} all-to-all(f32[32,8,128]{2,1,0:T(8,128)S(1)} %finish.1), channel_id=1, replica_groups=mesh['y'=4,'x'=4,'core'=2,'cluster'=8] {'y','x','core'}, dimensions={0} | all-to-all | bytes 262144 | tf_op jit(solution)/shard_map/all_to_all | solution.py:361
  138.9 0.8 place.1
Async XLA Ops:
  93.8 5.5 %collective-permute-start = (f32[512,1024]{1,0:T(8,128)S(1)}, f32[512,1024]{1,0:T(8,128)S(1)}, u32[]{:S(2)}, u32[]{:S(2)}) collective-permute-start(f32[512,1024]{1,0:T(8,128)S(1)} %sums.2), channel_id=1, source_target_pairs={{0,8},{8,0},{1,9},{9,1},{2,10},{10,2},{3,11},{11,3},{4,12},{12,4},... | collective-permute-start | bytes 6291464 | tf_op jit(solution)/shard_map/ppermute | solution.py:315
  99.6 15.2 %collective-permute-start.1 = (f32[128,1024]{1,0:T(8,128)S(1)}, f32[128,1024]{1,0:T(8,128)S(1)}, u32[]{:S(2)}, u32[]{:S(2)}) collective-permute-start(f32[128,1024]{1,0:T(8,128)S(1)} %get-tuple-element.28), channel_id=1, source_target_pairs={{0,16},{8,72},{16,32},{24,88},{32,48},{40,104},{48,0},{56,120},{64... | collective-permute-start | bytes 1572872 | tf_op jit(solution)/shard_map/ppermute | solution.py:339
  100.0 14.8 %collective-permute-start.2 = (f32[128,1024]{1,0:T(8,128)S(1)}, f32[128,1024]{1,0:T(8,128)S(1)}, u32[]{:S(2)}, u32[]{:S(2)}) collective-permute-start(f32[128,1024]{1,0:T(8,128)S(1)} %get-tuple-element.29), channel_id=1, source_target_pairs={{0,48},{8,200},{16,0},{24,216},{32,16},{40,232},{48,32},{56,248},{... | collective-permute-start | bytes 1572872 | tf_op jit(solution)/shard_map/ppermute | solution.py:339
  102.3 12.5 %collective-permute-start.3 = (f32[128,1024]{1,0:T(8,128)S(1)}, f32[128,1024]{1,0:T(8,128)S(1)}, u32[]{:S(2)}, u32[]{:S(2)}) collective-permute-start(f32[128,1024]{1,0:T(8,128)S(1)} %get-tuple-element.30), channel_id=1, source_target_pairs={{0,32},{8,136},{16,48},{24,152},{32,0},{40,168},{48,16},{56,184},{... | collective-permute-start | bytes 1572872 | tf_op jit(solution)/shard_map/ppermute | solution.py:339
  114.9 5.1 %collective-permute-start.4 = (f32[32,1024]{1,0:T(8,128)S(1)}, f32[32,1024]{1,0:T(8,128)S(1)}, u32[]{:S(2)}, u32[]{:S(2)}) collective-permute-start(f32[32,1024]{1,0:T(8,128)S(1)} %get-tuple-element.32), channel_id=1, source_target_pairs={{0,64},{8,24},{16,80},{24,40},{32,96},{40,56},{48,112},{56,8},{64,... | collective-permute-start | bytes 393224 | tf_op jit(solution)/shard_map/ppermute | solution.py:339
  115.2 5.8 %collective-permute-start.5 = (f32[32,1024]{1,0:T(8,128)S(1)}, f32[32,1024]{1,0:T(8,128)S(1)}, u32[]{:S(2)}, u32[]{:S(2)}) collective-permute-start(f32[32,1024]{1,0:T(8,128)S(1)} %get-tuple-element.33), channel_id=1, source_target_pairs={{0,192},{8,56},{16,208},{24,8},{32,224},{40,24},{48,240},{56,40},{... | collective-permute-start | bytes 393224 | tf_op jit(solution)/shard_map/ppermute | solution.py:339
  117.7 5.3 %collective-permute-start.6 = (f32[32,1024]{1,0:T(8,128)S(1)}, f32[32,1024]{1,0:T(8,128)S(1)}, u32[]{:S(2)}, u32[]{:S(2)}) collective-permute-start(f32[32,1024]{1,0:T(8,128)S(1)} %get-tuple-element.34), channel_id=1, source_target_pairs={{0,128},{8,40},{16,144},{24,56},{32,160},{40,8},{48,176},{56,24},{... | collective-permute-start | bytes 393224 | tf_op jit(solution)/shard_map/ppermute | solution.py:339

commit v3 on v2

--- a/solution.py
+++ b/solution.py
@@ -60,38 +60,66 @@
         out_ref[copy] = total
 
 
-def prepare_kernel(order, embeddings_ref, centroids_ref, kernel_ref, unit_ref, column_ref, centroid_scratch, partial):
-    step = pl.program_id(0)
-    chunk = embeddings_ref.shape[0]
+def prepare_kernel(
+    order, chunk, embeddings_ref, centroids_ref, kernel_ref, unit_ref, column_ref,
+    raw_rows, raw_centroids, unit_centroids, even_rows, odd_rows, even_cosine, odd_cosine, partial, arrived,
+):
     share = centroids_ref.shape[0] // len(order)
-
-    @pl.when(step == 0)
-    def _():
-        for place, block in enumerate(order):
-            centroid_scratch[place * share : (place + 1) * share, :] = unit(
-                centroids_ref[block * share : (block + 1) * share, :]
-            )
-        partial[...] = jnp.zeros_like(partial)
-
-    unit_rows = unit(embeddings_ref[...])
-    start = pl.multiple_of(step * chunk, chunk)
-    unit_ref[pl.ds(start, chunk), :] = unit_rows
-    height = 256
-    for part in range(centroid_scratch.shape[0] // height):
-        rows = slice(part * height, (part + 1) * height)
-        cosine = lax.dot_general(
-            centroid_scratch[rows, :], unit_rows, (((1,), (1,)), ((), ())), preferred_element_type=jnp.float32
+    chunks = embeddings_ref.shape[0] // chunk
+
+    copies = [
+        pltpu.make_async_copy(centroids_ref, raw_centroids, arrived.at[0]),
+        pltpu.make_async_copy(embeddings_ref, raw_rows, arrived.at[1]),
+    ]
+    for copy in copies:
+        copy.start()
+
+    def normalise(index, out_ref):
+        start = pl.multiple_of(index * chunk, chunk)
+        rows = unit(raw_rows[pl.ds(start, chunk), :])
+        out_ref[...] = rows
+        unit_ref[pl.ds(start, chunk), :] = rows
+
+    def product(rows_ref, out_ref):
+        out_ref[...] = lax.dot_general(
+            unit_centroids[...], rows_ref[...], (((1,), (1,)), ((), ())), preferred_element_type=jnp.float32
         )
-        affinity = jnp.exp2((cosine - 1.0) * EXPONENT_SLOPE)
-        kernel_ref[rows, pl.ds(start, chunk)] = affinity
+
+    def exponential(index, cosine_ref):
+        start = pl.multiple_of(index * chunk, chunk)
+        affinity = jnp.exp2((cosine_ref[...] - 1.0) * EXPONENT_SLOPE)
+        kernel_ref[:, pl.ds(start, chunk)] = affinity
         folded = affinity[:, :LANES]
         for tile in range(1, chunk // LANES):
             folded = folded + affinity[:, tile * LANES : (tile + 1) * LANES]
-        partial[rows, :] += folded
-
-    @pl.when(step == pl.num_programs(0) - 1)
-    def _():
-        to_lanes(partial, column_ref)
+        partial[...] += folded
+
+    copies[0].wait()
+    for place, block in enumerate(order):
+        unit_centroids[place * share : (place + 1) * share, :] = unit(
+            raw_centroids[block * share : (block + 1) * share, :]
+        )
+    partial[...] = jnp.zeros_like(partial)
+    copies[1].wait()
+    normalise(0, even_rows)
+    product(even_rows, even_cosine)
+    normalise(1, odd_rows)
+
+    def body(pair, carry):
+        index = 2 * pair
+        product(odd_rows, odd_cosine)
+        exponential(index, even_cosine)
+        normalise(index + 2, even_rows)
+        product(even_rows, even_cosine)
+        exponential(index + 1, odd_cosine)
+        normalise(index + 3, odd_rows)
+        return carry
+
+    lax.fori_loop(0, chunks // 2 - 1, body, 0)
+    product(odd_rows, odd_cosine)
+    exponential(chunks - 2, even_cosine)
+    exponential(chunks - 1, odd_cosine)
+    to_lanes(partial, column_ref)
 
 
 def row_kernel(target, columns_ref, kernel_ref, row_ref, scale_scratch):
@@ -151,8 +179,8 @@
         ).astype(jnp.bfloat16)
 
 
-def sums_kernel(counts, given, rows_ref, kernel_ref, unit_ref, *rest):
-    outs, weight_scratch = rest[:-1], rest[-1]
+def sums_kernel(counts, given, distances, rows_ref, kernel_ref, unit_ref, *rest):
+    received, outs, weight_scratch = rest[: -1 - len(distances)], rest[-1 - len(distances) : -1], rest[-1]
     slow, fast = counts
     half = slow * fast
     share = kernel_ref.shape[0] // (2 * half)
@@ -160,27 +188,16 @@
     y, x, core = (lax.axis_index(name) for name in ROWS_DP)
     base = 1 - core if given else core
     first, second = jnp.where(base == 0, x, y), jnp.where(base == 0, y, x)
-    for a in range(slow):
+    height = fast * share
+    for part, a in enumerate(distances):
         for b in range(fast):
-            place = a * fast + b
             block = base * half + lax.rem(first + a, slow) * fast + lax.rem(second + b, fast)
-            weigh(kernel_ref, scale, weight_scratch, pl.multiple_of(block * share, share), place, share)
-    height = fast * share
-    if len(outs) == 1:
-        outs[0][...] = jnp.dot(weight_scratch[...], unit_ref[...], preferred_element_type=jnp.float32)
-    else:
-        for a in range(slow):
-            outs[a][...] = jnp.dot(
-                weight_scratch[a * height : (a + 1) * height, :], unit_ref[...], preferred_element_type=jnp.float32
-            )
-
-
-def add_kernel(parts, *refs):
-    received_ref = refs[0]
-    kept, outs = refs[1 : 1 + parts], refs[1 + parts :]
-    height = kept[0].shape[0]
-    for part in range(parts):
-        outs[part][...] = kept[part][...] + received_ref[part * height : (part + 1) * height, :]
+            weigh(kernel_ref, scale, weight_scratch, pl.multiple_of(block * share, share), part * fast + b, share)
+    for part in range(len(distances)):
+        sums = jnp.dot(
+            weight_scratch[part * height : (part + 1) * height, :], unit_ref[...], preferred_element_type=jnp.float32
+        )
+        outs[part][...] = sums + received[part][...] if received else sums
 
 
 def fold_kernel(parts, *refs):
@@ -246,23 +263,29 @@
     target = rows * owners / (local * clusters)
     order = share_order(chips_y, chips_x, share)
     f32, bf16 = jnp.float32, jnp.bfloat16
-    chunk = 256
+    chunk = 512
 
     kernel, unit_rows, columns = pl.pallas_call(
-        functools.partial(prepare_kernel, order),
-        grid=(rows // chunk,),
-        in_specs=[
-            pl.BlockSpec((chunk, width), lambda i: (i, 0)),
-            pl.BlockSpec((local, width), lambda i: (0, 0)),
-        ],
+        functools.partial(prepare_kernel, order, chunk),
+        in_specs=[pl.BlockSpec(memory_space=pltpu.HBM)] * 2,
         out_specs=[VMEM, VMEM, VMEM],
         out_shape=[
             pltpu.VMEM((local, rows), f32),
             pltpu.VMEM((rows, width), bf16),
             pltpu.VMEM((owners, local // LANES, LANES), f32),
         ],
-        scratch_shapes=[pltpu.VMEM((local, width), bf16), pltpu.VMEM((local, LANES), f32)],
-        compiler_params=params(16),
+        scratch_shapes=[
+            pltpu.VMEM((rows, width), bf16),
+            pltpu.VMEM((local, width), bf16),
+            pltpu.VMEM((local, width), bf16),
+            pltpu.VMEM((chunk, width), bf16),
+            pltpu.VMEM((chunk, width), bf16),
+            pltpu.VMEM((local, chunk), f32),
+            pltpu.VMEM((local, chunk), f32),
+            pltpu.VMEM((local, LANES), f32),
+            pltpu.SemaphoreType.DMA((2,)),
+        ],
+        compiler_params=params(24),
         name="prepare",
     )(streamed(embeddings), streamed(centroids))
 
@@ -295,51 +318,58 @@
         )(resident(columns), resident(kernel))
         row_sums = row_exchange(row_sums)
 
-    half = owners // cores * share
-
-    def weighted(given, parts):
+    height = chips_y * share
+
+    def weighted(row_sums, given, distances, received=()):
+        count = len(distances)
         return pl.pallas_call(
-            functools.partial(sums_kernel, (chips_x, chips_y), given),
-            in_specs=[VMEM] * 3,
-            out_specs=[VMEM] * parts,
-            out_shape=[pltpu.VMEM((half // parts, width), f32)] * parts,
-            scratch_shapes=[pltpu.VMEM((half, rows), bf16)],
-            compiler_params=params(8),
+            functools.partial(sums_kernel, (chips_x, chips_y), given, distances),
+            in_specs=[VMEM] * (3 + len(received)),
+            out_specs=[VMEM] * count,
+            out_shape=[pltpu.VMEM((height, width), f32)] * count,
+            scratch_shapes=[pltpu.VMEM((count * height, rows), bf16)],
+            compiler_params=params(6),
             cost_estimate=pl.CostEstimate(
-                flops=2 * half * rows * width, bytes_accessed=4 * half * (rows + width), transcendentals=0
+                flops=2 * count * height * rows * width,
+                bytes_accessed=4 * count * height * (rows + width),
+                transcendentals=0,
             ),
             name="sums",
-        )(resident(row_sums), resident(kernel), resident(unit_rows))
-
-    (given,) = weighted(True, 1)
-    received = lax.ppermute(given, "core", ring(2, 1))
-    kept = weighted(False, chips_x)
-
-    first_parts = pl.pallas_call(
-        functools.partial(add_kernel, chips_x),
-        in_specs=[VMEM] * (1 + chips_x),
-        out_specs=[VMEM] * chips_x,
-        out_shape=[pltpu.VMEM((half // chips_x, width), f32)] * chips_x,
-        compiler_params=params(),
-        name="cores",
-    )(resident(received), *[resident(part) for part in kept])
-
-    def stage(parts, x_core):
-        got = [parts[0]]
-        for k in (1, 3, 2):
-            pairs = []
-            for j in range(chips_y):
-                for i in range(chips_x):
-                    for c in range(cores):
-                        if c == x_core:
-                            to = (j * chips_x + (i + k) % chips_x) * cores + c
-                        else:
-                            to = ((j + k) % chips_y * chips_x + i) * cores + c
-                        pairs.append(((j * chips_x + i) * cores + c, to))
-            got.append(lax.ppermute(parts[k], ROWS_DP, pairs))
-        return got
-
-    got = stage(first_parts, 0)
+        )(resident(row_sums), resident(kernel), resident(unit_rows), *[resident(part) for part in received])
+
+    def swap(parts):
+        return [lax.ppermute(part, "core", ring(2, 1)) for part in parts]
+
+    def hop(part, k, x_core):
+        pairs = []
+        for j in range(chips_y):
+            for i in range(chips_x):
+                for c in range(cores):
+                    if c == x_core:
+                        to = (j * chips_x + (i + k) % chips_x) * cores + c
+                    else:
+                        to = ((j + k) % chips_y * chips_x + i) * cores + c
+                    pairs.append(((j * chips_x + i) * cores + c, to))
+        return lax.ppermute(part, ROWS_DP, pairs)
+
+    def after(value, *others):
+        return lax.optimization_barrier((value,) + others)[0]
+
+    far = weighted(row_sums, True, (2,))
+    row_sums = after(row_sums, *far)
+    far = swap(far)
+    near = weighted(row_sums, True, (1, 3))
+    (part_2,) = weighted(row_sums, False, (2,), far)
+    got_2 = hop(part_2, 2, 0)
+    near = swap([after(part, part_2) for part in near])
+    row_sums = after(row_sums, part_2)
+    own = weighted(row_sums, True, (0,))
+    part_1, part_3 = weighted(row_sums, False, (1, 3), near)
+    got_1, got_3 = hop(part_1, 1, 0), hop(part_3, 3, 0)
+    row_sums = after(row_sums, part_1)
+    own = swap([after(part, part_1) for part in own])
+    part_0 = weighted(row_sums, False, (0,))
+    got = [*part_0, *own, got_2, got_1, got_3]
     second_parts = pl.pallas_call(
         functools.partial(fold_kernel, chips_y),
         in_specs=[VMEM] * len(got),
@@ -348,7 +378,7 @@
         compiler_params=params(),
         name="fold",
     )(*[resident(part) for part in got])
-    got = stage(second_parts, 1)
+    got = [second_parts[0]] + [hop(second_parts[k], k, 1) for k in (1, 3, 2)]
     tiles = pl.pallas_call(
         finish_kernel,
         in_specs=[VMEM] * len(got),

time: 140 us -> 133 us (0.950)
  waiting for transfers between devices: 19.2 us -> 14.6 us
  blocking collectives: 91 us -> 89 us
  Pallas kernels: 22.1 us -> 20.2 us
  starting transfers between devices: 7.24 us -> 8.95 us
    ppermute x7 -> x10, waiting for transfers between devices: 19.2 us -> 14.6 us  [the longest x6 14 us: hop(): return lax.ppermute(part, ROWS_DP, pairs)]
    all_to_all x1, blocking collectives: 15.6 us -> 13.5 us  [per_device(): tiles = lax.all_to_all(tiles, ROWS_DP, 0, 0)]
    pallas_call x4 -> x7, Pallas kernels: 15.5 us -> 13.6 us  [the longest x1 8.18 us: per_device(): pl.pallas_call(functools.partial(prepare_kernel, order, chunk), in_specs=...]
    ppermute x7 -> x10, starting transfers between devices: 7.24 us -> 8.95 us  [the longest x6 5.67 us: hop(): return lax.ppermute(part, ROWS_DP, pairs)]
  transfers between devices with their start and end apart: 7 -> 10, of which waited for: 5 -> 7; matrix products, arithmetic and copies ran while one was open for 0% -> 0% of each run, Pallas kernels for 2% -> 3%
where the time goes in v3:
time: 133 us
  blocking collectives  89 us (67%)
  Pallas kernels  20.2 us (15%)
  waiting for transfers between devices  14.6 us (11%)
  starting transfers between devices  8.95 us (7%)
    all_to_all x3, blocking collectives, column_exchange(): return lax.all_to_all(sums, ROWS_DP, 0, 0)  41.2 us
    all_to_all x3, blocking collectives, row_exchange(): return lax.all_to_all(sums, 'cluster', 0, 0)  34.3 us
    ppermute x6, waiting for transfers between devices, hop(): return lax.ppermute(part, ROWS_DP, pairs)  14 us
    all_to_all x1, blocking collectives, per_device(): tiles = lax.all_to_all(tiles, ROWS_DP, 0, 0)  13.5 us
    pallas_call x1, Pallas kernels, per_device(): pl.pallas_call(functools.partial(prepare_kernel, order, chunk), in_specs=...  8.18 us
    ppermute x6, starting transfers between devices, hop(): return lax.ppermute(part, ROWS_DP, pairs)  5.67 us
    pallas_call x6, Pallas kernels, weighted(): pl.pallas_call(functools.partial(sums_kernel, (chips_x, chips_y), given,...  5.42 us
    pallas_call x3, Pallas kernels, per_device(): pl.pallas_call(functools.partial(row_kernel, target), in_specs=[VMEM, VME...  3.29 us
  transfers between devices with their start and end apart: 10, of which 7 were waited for; matrix products, arithmetic and copies ran while one was open for 0% of the time, Pallas kernels for 3%

profile of v3, /device:TPU:1, one launch (start us, length us, event | category | flops | bytes accessed | tf_op | source)
XLA Modules:
  0.0 132.8 jit_solution(14669984232565843223)
XLA Ops:
  0.0 8.2 %prepare.1 = (f32[1024,2048]{1,0:T(8,128)S(1)}, bf16[2048,1024]{1,0:T(8,128)(2,1)S(1)}, f32[32,8,128]{2,1,0:T(8,128)S(1)}) custom-call(bf16[2048,1024]{1,0:T(8,128)(2,1)} %embeddings_ref.1, bf16[1024,1024]{1,0:T(8,128)(2,1)} %centroids_ref.1), custom_call_target="tpu_custom_call" | custom-call | tf_op jit(solution)/shard_map/prepare/pallas_call | solution.py:268
  8.2 16.0 %all_to_all.35.columns_ref = f32[32,8,128]{2,1,0:T(8,128)S(1)} all-to-all(f32[32,8,128]{2,1,0:T(8,128)S(1)} %get-tuple-element.22), channel_id=1, replica_groups=mesh['y'=4,'x'=4,'core'=2,'cluster'=8] {'y','x','core'}, dimensions={0} | all-to-all | bytes 262144 | tf_op jit(solution)/shard_map/all_to_all | solution.py:293
  24.2 1.1 rows.3
  25.3 15.2 %all_to_all.36.rows_ref = f32[8,16,128]{2,1,0:T(8,128)S(1)} all-to-all(f32[8,16,128]{2,1,0:T(8,128)S(1)} %rows.3), channel_id=1, replica_groups=mesh['y'=4,'x'=4,'core'=2,'cluster'=8] {'cluster'}, dimensions={0} | all-to-all | bytes 131072 | tf_op jit(solution)/shard_map/all_to_all | solution.py:296
  40.5 1.1 columns.2
  41.6 12.7 %all_to_all.37.columns_ref = f32[32,8,128]{2,1,0:T(8,128)S(1)} all-to-all(f32[32,8,128]{2,1,0:T(8,128)S(1)} %columns.2), channel_id=1, replica_groups=mesh['y'=4,'x'=4,'core'=2,'cluster'=8] {'y','x','core'}, dimensions={0} | all-to-all | bytes 262144 | tf_op jit(solution)/shard_map/all_to_all | solution.py:293
  54.3 1.1 rows.4
  55.4 9.5 %all_to_all.38.rows_ref = f32[8,16,128]{2,1,0:T(8,128)S(1)} all-to-all(f32[8,16,128]{2,1,0:T(8,128)S(1)} %rows.4), channel_id=1, replica_groups=mesh['y'=4,'x'=4,'core'=2,'cluster'=8] {'cluster'}, dimensions={0} | all-to-all | bytes 131072 | tf_op jit(solution)/shard_map/all_to_all | solution.py:296
  64.9 1.1 columns.3
  66.0 12.5 %all_to_all.39.columns_ref = f32[32,8,128]{2,1,0:T(8,128)S(1)} all-to-all(f32[32,8,128]{2,1,0:T(8,128)S(1)} %columns.3), channel_id=1, replica_groups=mesh['y'=4,'x'=4,'core'=2,'cluster'=8] {'y','x','core'}, dimensions={0} | all-to-all | bytes 262144 | tf_op jit(solution)/shard_map/all_to_all | solution.py:293
  78.5 1.1 rows.5
  79.6 9.5 %all_to_all.40.rows_ref = f32[8,16,128]{2,1,0:T(8,128)S(1)} all-to-all(f32[8,16,128]{2,1,0:T(8,128)S(1)} %rows.5), channel_id=1, replica_groups=mesh['y'=4,'x'=4,'core'=2,'cluster'=8] {'cluster'}, dimensions={0} | all-to-all | bytes 131072 | tf_op jit(solution)/shard_map/all_to_all | solution.py:296
  89.1 0.7 sums.6
  89.8 1.7 %collective-permute-start = (f32[128,1024]{1,0:T(8,128)S(1)}, f32[128,1024]{1,0:T(8,128)S(1)}, u32[]{:S(2)}, u32[]{:S(2)}) collective-permute-start(f32[128,1024]{1,0:T(8,128)S(1)} %sums.6), channel_id=1, source_target_pairs={{0,8},{8,0},{1,9},{9,1},{2,10},{10,2},{3,11},{11,3},{4,12},{12,4},... | collective-permute-start | bytes 1572872 | tf_op jit(solution)/shard_map/ppermute | solution.py:341
  91.6 1.3 sums.8
  92.8 0.3 collective-permute-done.rest_0_
  93.1 0.7 sums.7
  93.8 0.5 collective-permute-start.1
  94.3 0.3 collective-permute-start.2
  94.6 1.0 collective-permute-start.4
  95.5 0.7 sums.11
  96.3 0.0 collective-permute-done.1.rest_0_
  96.3 0.3 collective-permute-done.2.rest_1_
  96.6 1.3 sums.9
  97.9 0.4 collective-permute-start.5
  98.3 0.8 collective-permute-start.3
  99.1 1.6 %collective-permute-start.6 = (f32[128,1024]{1,0:T(8,128)S(1)}, f32[128,1024]{1,0:T(8,128)S(1)}, u32[]{:S(2)}, u32[]{:S(2)}) collective-permute-start(f32[128,1024]{1,0:T(8,128)S(1)} %get-tuple-element.34), channel_id=1, source_target_pairs={{0,48},{8,200},{16,0},{24,216},{32,16},{40,232},{48,32},{56,248},{... | collective-permute-start | bytes 1572872 | tf_op jit(solution)/shard_map/ppermute | solution.py:353
  100.6 0.7 sums.10.refs_0_
  101.3 3.1 %collective-permute-done.4.refs_2_ = f32[128,1024]{1,0:T(8,128)S(1)} collective-permute-done((f32[128,1024]{1,0:T(8,128)S(1)}, f32[128,1024]{1,0:T(8,128)S(1)}, u32[]{:S(2)}, u32[]{:S(2)}) %collective-permute-start.4) | collective-permute-done | bytes 524320 | tf_op jit(solution)/shard_map/ppermute | solution.py:353
  104.4 0.0 collective-permute-done.3.refs_1_
  104.4 5.6 %collective-permute-done.5.refs_3_ = f32[128,1024]{1,0:T(8,128)S(1)} collective-permute-done((f32[128,1024]{1,0:T(8,128)S(1)}, f32[128,1024]{1,0:T(8,128)S(1)}, u32[]{:S(2)}, u32[]{:S(2)}) %collective-permute-start.5) | collective-permute-done | bytes 524320 | tf_op jit(solution)/shard_map/ppermute | solution.py:353
  110.0 0.0 collective-permute-done.6.refs_4_
  110.0 0.1 fold.1
  110.1 0.1 collective-permute-start.7
  110.3 2.6 %collective-permute-start.8 = (f32[32,1024]{1,0:T(8,128)S(1)}, f32[32,1024]{1,0:T(8,128)S(1)}, u32[]{:S(2)}, u32[]{:S(2)}) collective-permute-start(f32[32,1024]{1,0:T(8,128)S(1)} %get-tuple-element.37), channel_id=1, source_target_pairs={{0,192},{8,56},{16,208},{24,8},{32,224},{40,24},{48,240},{56,40},{... | collective-permute-start | bytes 393224 | tf_op jit(solution)/shard_map/ppermute | solution.py:353
  112.9 0.0 collective-permute-start.9
  112.9 2.3 %collective-permute-done.7.refs_1_ = f32[32,1024]{1,0:T(8,128)S(1)} collective-permute-done((f32[32,1024]{1,0:T(8,128)S(1)}, f32[32,1024]{1,0:T(8,128)S(1)}, u32[]{:S(2)}, u32[]{:S(2)}) %collective-permute-start.7) | collective-permute-done | bytes 131104 | tf_op jit(solution)/shard_map/ppermute | solution.py:353
  115.3 1.0 collective-permute-done.8.refs_2_
  116.2 2.0 %collective-permute-done.9.refs_3_ = f32[32,1024]{1,0:T(8,128)S(1)} collective-permute-done((f32[32,1024]{1,0:T(8,128)S(1)}, f32[32,1024]{1,0:T(8,128)S(1)}, u32[]{:S(2)}, u32[]{:S(2)}) %collective-permute-start.9) | collective-permute-done | bytes 131104 | tf_op jit(solution)/shard_map/ppermute | solution.py:353
  118.2 0.3 finish.1
  118.5 13.5 %all_to_all.41.tiles_ref = f32[32,8,128]{2,1,0:T(8,128)S(1)} all-to-all(f32[32,8,128]{2,1,0:T(8,128)S(1)} %finish.1), channel_id=1, replica_groups=mesh['y'=4,'x'=4,'core'=2,'cluster'=8] {'y','x','core'}, dimensions={0} | all-to-all | bytes 262144 | tf_op jit(solution)/shard_map/all_to_all | solution.py:391
  132.0 0.8 place.1
Async XLA Ops:
  89.8 3.3 %collective-permute-start = (f32[128,1024]{1,0:T(8,128)S(1)}, f32[128,1024]{1,0:T(8,128)S(1)}, u32[]{:S(2)}, u32[]{:S(2)}) collective-permute-start(f32[128,1024]{1,0:T(8,128)S(1)} %sums.6), channel_id=1, source_target_pairs={{0,8},{8,0},{1,9},{9,1},{2,10},{10,2},{3,11},{11,3},{4,12},{12,4},... | collective-permute-start | bytes 1572872 | tf_op jit(solution)/shard_map/ppermute | solution.py:341
  93.8 2.4 %collective-permute-start.1 = (f32[128,1024]{1,0:T(8,128)S(1)}, f32[128,1024]{1,0:T(8,128)S(1)}, u32[]{:S(2)}, u32[]{:S(2)}) collective-permute-start(f32[128,1024]{1,0:T(8,128)S(1)} %get-tuple-element.28), channel_id=1, source_target_pairs={{0,8},{8,0},{1,9},{9,1},{2,10},{10,2},{3,11},{11,3},{4,12},{12,4},... | collective-permute-start | bytes 1572872 | tf_op jit(solution)/shard_map/ppermute | solution.py:341
  94.3 2.3 %collective-permute-start.2 = (f32[128,1024]{1,0:T(8,128)S(1)}, f32[128,1024]{1,0:T(8,128)S(1)}, u32[]{:S(2)}, u32[]{:S(2)}) collective-permute-start(f32[128,1024]{1,0:T(8,128)S(1)} %get-tuple-element.30), channel_id=1, source_target_pairs={{0,8},{8,0},{1,9},{9,1},{2,10},{10,2},{3,11},{11,3},{4,12},{12,4},... | collective-permute-start | bytes 1572872 | tf_op jit(solution)/shard_map/ppermute | solution.py:341
  94.6 9.9 %collective-permute-start.4 = (f32[128,1024]{1,0:T(8,128)S(1)}, f32[128,1024]{1,0:T(8,128)S(1)}, u32[]{:S(2)}, u32[]{:S(2)}) collective-permute-start(f32[128,1024]{1,0:T(8,128)S(1)} %sums.7), channel_id=1, source_target_pairs={{0,32},{8,136},{16,48},{24,152},{32,0},{40,168},{48,16},{56,184},{... | collective-permute-start | bytes 1572872 | tf_op jit(solution)/shard_map/ppermute | solution.py:353
  97.9 12.2 %collective-permute-start.5 = (f32[128,1024]{1,0:T(8,128)S(1)}, f32[128,1024]{1,0:T(8,128)S(1)}, u32[]{:S(2)}, u32[]{:S(2)}) collective-permute-start(f32[128,1024]{1,0:T(8,128)S(1)} %get-tuple-element.31), channel_id=1, source_target_pairs={{0,16},{8,72},{16,32},{24,88},{32,48},{40,104},{48,0},{56,120},{64... | collective-permute-start | bytes 1572872 | tf_op jit(solution)/shard_map/ppermute | solution.py:353
  98.3 6.2 %collective-permute-start.3 = (f32[128,1024]{1,0:T(8,128)S(1)}, f32[128,1024]{1,0:T(8,128)S(1)}, u32[]{:S(2)}, u32[]{:S(2)}) collective-permute-start(f32[128,1024]{1,0:T(8,128)S(1)} %sums.11), channel_id=1, source_target_pairs={{0,8},{8,0},{1,9},{9,1},{2,10},{10,2},{3,11},{11,3},{4,12},{12,4},... | collective-permute-start | bytes 1572872 | tf_op jit(solution)/shard_map/ppermute | solution.py:341
  99.1 11.0 %collective-permute-start.6 = (f32[128,1024]{1,0:T(8,128)S(1)}, f32[128,1024]{1,0:T(8,128)S(1)}, u32[]{:S(2)}, u32[]{:S(2)}) collective-permute-start(f32[128,1024]{1,0:T(8,128)S(1)} %get-tuple-element.34), channel_id=1, source_target_pairs={{0,48},{8,200},{16,0},{24,216},{32,16},{40,232},{48,32},{56,248},{... | collective-permute-start | bytes 1572872 | tf_op jit(solution)/shard_map/ppermute | solution.py:353
  110.1 5.1 %collective-permute-start.7 = (f32[32,1024]{1,0:T(8,128)S(1)}, f32[32,1024]{1,0:T(8,128)S(1)}, u32[]{:S(2)}, u32[]{:S(2)}) collective-permute-start(f32[32,1024]{1,0:T(8,128)S(1)} %get-tuple-element.36), channel_id=1, source_target_pairs={{0,64},{8,24},{16,80},{24,40},{32,96},{40,56},{48,112},{56,8},{64,... | collective-permute-start | bytes 393224 | tf_op jit(solution)/shard_map/ppermute | solution.py:353
  110.3 6.0 %collective-permute-start.8 = (f32[32,1024]{1,0:T(8,128)S(1)}, f32[32,1024]{1,0:T(8,128)S(1)}, u32[]{:S(2)}, u32[]{:S(2)}) collective-permute-start(f32[32,1024]{1,0:T(8,128)S(1)} %get-tuple-element.37), channel_id=1, source_target_pairs={{0,192},{8,56},{16,208},{24,8},{32,224},{40,24},{48,240},{56,40},{... | collective-permute-start | bytes 393224 | tf_op jit(solution)/shard_map/ppermute | solution.py:353
  112.9 5.3 %collective-permute-start.9 = (f32[32,1024]{1,0:T(8,128)S(1)}, f32[32,1024]{1,0:T(8,128)S(1)}, u32[]{:S(2)}, u32[]{:S(2)}) collective-permute-start(f32[32,1024]{1,0:T(8,128)S(1)} %get-tuple-element.38), channel_id=1, source_target_pairs={{0,128},{8,40},{16,144},{24,56},{32,160},{40,8},{48,176},{56,24},{... | collective-permute-start | bytes 393224 | tf_op jit(solution)/shard_map/ppermute | solution.py:353

commit v4 on v3

--- a/solution.py
+++ b/solution.py
@@ -67,12 +67,15 @@
     share = centroids_ref.shape[0] // len(order)
     chunks = embeddings_ref.shape[0] // chunk
 
-    copies = [
-        pltpu.make_async_copy(centroids_ref, raw_centroids, arrived.at[0]),
-        pltpu.make_async_copy(embeddings_ref, raw_rows, arrived.at[1]),
-    ]
-    for copy in copies:
-        copy.start()
+    def fetch(start, size, which):
+        rows = pl.ds(start, size)
+        return pltpu.make_async_copy(embeddings_ref.at[rows, :], raw_rows.at[rows, :], arrived.at[which])
+
+    fetch_centroids = pltpu.make_async_copy(centroids_ref, raw_centroids, arrived.at[0])
+    fetch_first = fetch(0, chunk, 1)
+    fetch_rest = fetch(chunk, embeddings_ref.shape[0] - chunk, 2)
+    fetch_centroids.start()
+    fetch_first.start()
 
     def normalise(index, out_ref):
         start = pl.multiple_of(index * chunk, chunk)
@@ -94,15 +97,17 @@
             folded = folded + affinity[:, tile * LANES : (tile + 1) * LANES]
         partial[...] += folded
 
-    copies[0].wait()
+    fetch_centroids.wait()
+    fetch_rest.start()
     for place, block in enumerate(order):
         unit_centroids[place * share : (place + 1) * share, :] = unit(
             raw_centroids[block * share : (block + 1) * share, :]
         )
     partial[...] = jnp.zeros_like(partial)
-    copies[1].wait()
+    fetch_first.wait()
     normalise(0, even_rows)
     product(even_rows, even_cosine)
+    fetch_rest.wait()
     normalise(1, odd_rows)
 
     def body(pair, carry):
@@ -141,9 +146,8 @@
             out.append(sums[tile] + jnp.sum(product.reshape(height // SUBLANES, SUBLANES, LANES), axis=0))
         return tuple(out)
 
-    sums = lax.fori_loop(
-        0, centroids // height, body, tuple(jnp.zeros((SUBLANES, LANES), jnp.float32) for _ in range(tiles))
-    )
+    nothing = tuple(jnp.zeros((SUBLANES, LANES), jnp.float32) for _ in range(tiles))
+    sums = lax.fori_loop(0, centroids // height, body, nothing, unroll=8)
     total = jnp.concatenate([jnp.sum(tile, axis=0, keepdims=True) for tile in sums], axis=0)
     for copy in range(row_ref.shape[0]):
         row_ref[copy] = total
@@ -166,7 +170,7 @@
         partial[pl.ds(start, height), :] = total.reshape(height, LANES)
         return carry
 
-    lax.fori_loop(0, centroids // height, body, 0)
+    lax.fori_loop(0, centroids // height, body, 0, unroll=8)
     to_lanes(partial, column_ref)
 
 
@@ -180,7 +184,7 @@
 
 
 def sums_kernel(counts, given, distances, rows_ref, kernel_ref, unit_ref, *rest):
-    received, outs, weight_scratch = rest[: -1 - len(distances)], rest[-1 - len(distances) : -1], rest[-1]
+    received, (out_ref, weight_scratch) = rest[:-2], rest[-2:]
     slow, fast = counts
     half = slow * fast
     share = kernel_ref.shape[0] // (2 * half)
@@ -188,16 +192,22 @@
     y, x, core = (lax.axis_index(name) for name in ROWS_DP)
     base = 1 - core if given else core
     first, second = jnp.where(base == 0, x, y), jnp.where(base == 0, y, x)
-    height = fast * share
     for part, a in enumerate(distances):
         for b in range(fast):
             block = base * half + lax.rem(first + a, slow) * fast + lax.rem(second + b, fast)
             weigh(kernel_ref, scale, weight_scratch, pl.multiple_of(block * share, share), part * fast + b, share)
-    for part in range(len(distances)):
-        sums = jnp.dot(
-            weight_scratch[part * height : (part + 1) * height, :], unit_ref[...], preferred_element_type=jnp.float32
-        )
-        outs[part][...] = sums + received[part][...] if received else sums
+    height = 128
+    for part in range(weight_scratch.shape[0] // height):
+        rows = slice(part * height, (part + 1) * height)
+        sums = jnp.dot(weight_scratch[rows, :], unit_ref[...], preferred_element_type=jnp.float32)
+        out_ref[rows, :] = sums + received[0][rows, :] if received else sums
+
+
+def add_kernel(own_ref, other_ref, *outs):
+    height = outs[0].shape[0]
+    for part, out_ref in enumerate(outs):
+        rows = slice(part * height, (part + 1) * height)
+        out_ref[...] = own_ref[rows, :] + other_ref[rows, :]
 
 
 def fold_kernel(parts, *refs):
@@ -283,7 +293,7 @@
             pltpu.VMEM((local, chunk), f32),
             pltpu.VMEM((local, chunk), f32),
             pltpu.VMEM((local, LANES), f32),
-            pltpu.SemaphoreType.DMA((2,)),
+            pltpu.SemaphoreType.DMA((3,)),
         ],
         compiler_params=params(24),
         name="prepare",
@@ -320,13 +330,13 @@
 
     height = chips_y * share
 
-    def weighted(row_sums, given, distances, received=()):
+    def weighted(row_sums, given, distances, *received):
         count = len(distances)
         return pl.pallas_call(
             functools.partial(sums_kernel, (chips_x, chips_y), given, distances),
             in_specs=[VMEM] * (3 + len(received)),
-            out_specs=[VMEM] * count,
-            out_shape=[pltpu.VMEM((height, width), f32)] * count,
+            out_specs=VMEM,
+            out_shape=pltpu.VMEM((count * height, width), f32),
             scratch_shapes=[pltpu.VMEM((count * height, rows), bf16)],
             compiler_params=params(6),
             cost_estimate=pl.CostEstimate(
@@ -337,8 +347,18 @@
             name="sums",
         )(resident(row_sums), resident(kernel), resident(unit_rows), *[resident(part) for part in received])
 
-    def swap(parts):
-        return [lax.ppermute(part, "core", ring(2, 1)) for part in parts]
+    def add(body, name, shapes, *arrays):
+        return pl.pallas_call(
+            body,
+            in_specs=[VMEM] * len(arrays),
+            out_specs=[VMEM] * len(shapes),
+            out_shape=[pltpu.VMEM(shape, f32) for shape in shapes],
+            compiler_params=params(),
+            name=name,
+        )(*[resident(array) for array in arrays])
+
+    def swap(part):
+        return lax.ppermute(part, "core", ring(2, 1))
 
     def hop(part, k, x_core):
         pairs = []
@@ -356,28 +376,25 @@
         return lax.optimization_barrier((value,) + others)[0]
 
     far = weighted(row_sums, True, (2,))
-    row_sums = after(row_sums, *far)
+    row_sums = after(row_sums, far)
     far = swap(far)
     near = weighted(row_sums, True, (1, 3))
-    (part_2,) = weighted(row_sums, False, (2,), far)
-    got_2 = hop(part_2, 2, 0)
-    near = swap([after(part, part_2) for part in near])
-    row_sums = after(row_sums, part_2)
+    row_sums = after(row_sums, near)
+    far = weighted(row_sums, False, (2,), far)
+    near = swap(after(near, far))
+    row_sums = after(row_sums, far)
+    far = hop(far, 2, 0)
+    near_own = weighted(row_sums, False, (1, 3))
+    up, down = add(add_kernel, "near", [(height, width)] * 2, near_own, near)
+    row_sums = after(row_sums, up)
+    up, down = hop(up, 1, 0), hop(down, 3, 0)
     own = weighted(row_sums, True, (0,))
-    part_1, part_3 = weighted(row_sums, False, (1, 3), near)
-    got_1, got_3 = hop(part_1, 1, 0), hop(part_3, 3, 0)
-    row_sums = after(row_sums, part_1)
-    own = swap([after(part, part_1) for part in own])
+    row_sums = after(row_sums, own)
+    own = swap(own)
     part_0 = weighted(row_sums, False, (0,))
-    got = [*part_0, *own, got_2, got_1, got_3]
-    second_parts = pl.pallas_call(
-        functools.partial(fold_kernel, chips_y),
-        in_specs=[VMEM] * len(got),
-        out_specs=[VMEM] * chips_y,
-        out_shape=[pltpu.VMEM((share, width), f32)] * chips_y,
-        compiler_params=params(),
-        name="fold",
-    )(*[resident(part) for part in got])
+    second_parts = add(
+        functools.partial(fold_kernel, chips_y), "fold", [(share, width)] * chips_y, part_0, own, far, up, down
+    )
     got = [second_parts[0]] + [hop(second_parts[k], k, 1) for k in (1, 3, 2)]
     tiles = pl.pallas_call(
         finish_kernel,

time: 133 us -> 131 us (0.985)
  Pallas kernels: 20.2 us -> 18.6 us
    ppermute x4 -> x3, starting transfers between devices: 3.28 us -> 3.32 us  [swap(): return lax.ppermute(part, 'core', ring(2, 1))]
  transfers between devices with their start and end apart: 10 -> 9, of which waited for: 7 -> 7; matrix products, arithmetic and copies ran while one was open for 0% -> 0% of each run, Pallas kernels for 3% -> 3%
where the time goes in v4:
time: 131 us
  blocking collectives  88.9 us (68%)
  Pallas kernels  18.6 us (14%)
  waiting for transfers between devices  14.3 us (11%)
  starting transfers between devices  9.03 us (7%)
    all_to_all x3, blocking collectives, column_exchange(): return lax.all_to_all(sums, ROWS_DP, 0, 0)  41.2 us
    all_to_all x3, blocking collectives, row_exchange(): return lax.all_to_all(sums, 'cluster', 0, 0)  34.3 us
    ppermute x6, waiting for transfers between devices, hop(): return lax.ppermute(part, ROWS_DP, pairs)  14 us
    all_to_all x1, blocking collectives, per_device(): tiles = lax.all_to_all(tiles, ROWS_DP, 0, 0)  13.4 us
    pallas_call x1, Pallas kernels, per_device(): pl.pallas_call(functools.partial(prepare_kernel, order, chunk), in_specs=...  7.79 us
    ppermute x6, starting transfers between devices, hop(): return lax.ppermute(part, ROWS_DP, pairs)  5.71 us
    pallas_call x6, Pallas kernels, weighted(): pl.pallas_call(functools.partial(sums_kernel, (chips_x, chips_y), given,...  5.42 us
    ppermute x3, starting transfers between devices, swap(): return lax.ppermute(part, 'core', ring(2, 1))  3.32 us
  transfers between devices with their start and end apart: 9, of which 7 were waited for; matrix products, arithmetic and copies ran while one was open for 0% of the time, Pallas kernels for 3%

profile of v4, /device:TPU:1, one launch (start us, length us, event | category | flops | bytes accessed | tf_op | source)
XLA Modules:
  0.0 130.9 jit_solution(10210402474145022894)
XLA Ops:
  0.0 7.8 %prepare.1 = (f32[1024,2048]{1,0:T(8,128)S(1)}, bf16[2048,1024]{1,0:T(8,128)(2,1)S(1)}, f32[32,8,128]{2,1,0:T(8,128)S(1)}) custom-call(bf16[2048,1024]{1,0:T(8,128)(2,1)} %embeddings_ref.1, bf16[1024,1024]{1,0:T(8,128)(2,1)} %centroids_ref.1), custom_call_target="tpu_custom_call" | custom-call | tf_op jit(solution)/shard_map/prepare/pallas_call | solution.py:278
  7.8 16.0 %all_to_all.35.columns_ref = f32[32,8,128]{2,1,0:T(8,128)S(1)} all-to-all(f32[32,8,128]{2,1,0:T(8,128)S(1)} %get-tuple-element.20), channel_id=1, replica_groups=mesh['y'=4,'x'=4,'core'=2,'cluster'=8] {'y','x','core'}, dimensions={0} | all-to-all | bytes 262144 | tf_op jit(solution)/shard_map/all_to_all | solution.py:303
  23.8 0.8 rows.3
  24.7 15.2 %all_to_all.36.rows_ref = f32[8,16,128]{2,1,0:T(8,128)S(1)} all-to-all(f32[8,16,128]{2,1,0:T(8,128)S(1)} %rows.3), channel_id=1, replica_groups=mesh['y'=4,'x'=4,'core'=2,'cluster'=8] {'cluster'}, dimensions={0} | all-to-all | bytes 131072 | tf_op jit(solution)/shard_map/all_to_all | solution.py:306
  39.9 0.8 columns.2
  40.7 12.7 %all_to_all.37.columns_ref = f32[32,8,128]{2,1,0:T(8,128)S(1)} all-to-all(f32[32,8,128]{2,1,0:T(8,128)S(1)} %columns.2), channel_id=1, replica_groups=mesh['y'=4,'x'=4,'core'=2,'cluster'=8] {'y','x','core'}, dimensions={0} | all-to-all | bytes 262144 | tf_op jit(solution)/shard_map/all_to_all | solution.py:303
  53.4 0.8 rows.4
  54.2 9.5 %all_to_all.38.rows_ref = f32[8,16,128]{2,1,0:T(8,128)S(1)} all-to-all(f32[8,16,128]{2,1,0:T(8,128)S(1)} %rows.4), channel_id=1, replica_groups=mesh['y'=4,'x'=4,'core'=2,'cluster'=8] {'cluster'}, dimensions={0} | all-to-all | bytes 131072 | tf_op jit(solution)/shard_map/all_to_all | solution.py:306
  63.7 0.8 columns.3
  64.5 12.5 %all_to_all.39.columns_ref = f32[32,8,128]{2,1,0:T(8,128)S(1)} all-to-all(f32[32,8,128]{2,1,0:T(8,128)S(1)} %columns.3), channel_id=1, replica_groups=mesh['y'=4,'x'=4,'core'=2,'cluster'=8] {'y','x','core'}, dimensions={0} | all-to-all | bytes 262144 | tf_op jit(solution)/shard_map/all_to_all | solution.py:303
  77.0 0.8 rows.5
  77.9 9.5 %all_to_all.40.rows_ref = f32[8,16,128]{2,1,0:T(8,128)S(1)} all-to-all(f32[8,16,128]{2,1,0:T(8,128)S(1)} %rows.5), channel_id=1, replica_groups=mesh['y'=4,'x'=4,'core'=2,'cluster'=8] {'cluster'}, dimensions={0} | all-to-all | bytes 131072 | tf_op jit(solution)/shard_map/all_to_all | solution.py:306
  87.4 0.7 sums.6
  88.1 1.9 %collective-permute-start = (f32[128,1024]{1,0:T(8,128)S(1)}, f32[128,1024]{1,0:T(8,128)S(1)}, u32[]{:S(2)}, u32[]{:S(2)}) collective-permute-start(f32[128,1024]{1,0:T(8,128)S(1)} %sums.6), channel_id=1, source_target_pairs={{0,8},{8,0},{1,9},{9,1},{2,10},{10,2},{3,11},{11,3},{4,12},{12,4},... | collective-permute-start | bytes 1572872 | tf_op jit(solution)/shard_map/ppermute | solution.py:361
  90.0 1.3 sums.7
  91.3 0.3 collective-permute-done.rest_0_
  91.6 0.7 sums.8
  92.3 0.5 collective-permute-start.1
  92.8 1.0 collective-permute-start.3
  93.7 1.3 sums.9.own_ref
  95.0 0.1 collective-permute-done.1.other_ref
  95.1 0.1 near.1
  95.2 0.5 collective-permute-start.4
  95.7 0.7 sums.10
  96.4 0.9 collective-permute-start.2
  97.3 1.5 %collective-permute-start.5 = (f32[128,1024]{1,0:T(8,128)S(1)}, f32[128,1024]{1,0:T(8,128)S(1)}, u32[]{:S(2)}, u32[]{:S(2)}) collective-permute-start(f32[128,1024]{1,0:T(8,128)S(1)} %get-tuple-element.30), channel_id=1, source_target_pairs={{0,48},{8,200},{16,0},{24,216},{32,16},{40,232},{48,32},{56,248},{... | collective-permute-start | bytes 1572872 | tf_op jit(solution)/shard_map/ppermute | solution.py:373
  98.8 0.7 sums.11.refs_0_
  99.6 3.1 %collective-permute-done.3.refs_2_ = f32[128,1024]{1,0:T(8,128)S(1)} collective-permute-done((f32[128,1024]{1,0:T(8,128)S(1)}, f32[128,1024]{1,0:T(8,128)S(1)}, u32[]{:S(2)}, u32[]{:S(2)}) %collective-permute-start.3) | collective-permute-done | bytes 524320 | tf_op jit(solution)/shard_map/ppermute | solution.py:373
  102.6 0.0 collective-permute-done.2.refs_1_
  102.6 5.6 %collective-permute-done.4.refs_3_ = f32[128,1024]{1,0:T(8,128)S(1)} collective-permute-done((f32[128,1024]{1,0:T(8,128)S(1)}, f32[128,1024]{1,0:T(8,128)S(1)}, u32[]{:S(2)}, u32[]{:S(2)}) %collective-permute-start.4) | collective-permute-done | bytes 524320 | tf_op jit(solution)/shard_map/ppermute | solution.py:373
  108.2 0.0 collective-permute-done.5.refs_4_
  108.2 0.1 fold.1
  108.3 0.1 collective-permute-start.6
  108.5 2.6 %collective-permute-start.7 = (f32[32,1024]{1,0:T(8,128)S(1)}, f32[32,1024]{1,0:T(8,128)S(1)}, u32[]{:S(2)}, u32[]{:S(2)}) collective-permute-start(f32[32,1024]{1,0:T(8,128)S(1)} %get-tuple-element.33), channel_id=1, source_target_pairs={{0,192},{8,56},{16,208},{24,8},{32,224},{40,24},{48,240},{56,40},{... | collective-permute-start | bytes 393224 | tf_op jit(solution)/shard_map/ppermute | solution.py:373
  111.1 0.0 collective-permute-start.8
  111.1 2.3 %collective-permute-done.6.refs_1_ = f32[32,1024]{1,0:T(8,128)S(1)} collective-permute-done((f32[32,1024]{1,0:T(8,128)S(1)}, f32[32,1024]{1,0:T(8,128)S(1)}, u32[]{:S(2)}, u32[]{:S(2)}) %collective-permute-start.6) | collective-permute-done | bytes 131104 | tf_op jit(solution)/shard_map/ppermute | solution.py:373
  113.4 1.0 collective-permute-done.7.refs_2_
  114.4 2.0 %collective-permute-done.8.refs_3_ = f32[32,1024]{1,0:T(8,128)S(1)} collective-permute-done((f32[32,1024]{1,0:T(8,128)S(1)}, f32[32,1024]{1,0:T(8,128)S(1)}, u32[]{:S(2)}, u32[]{:S(2)}) %collective-permute-start.8) | collective-permute-done | bytes 131104 | tf_op jit(solution)/shard_map/ppermute | solution.py:373
  116.4 0.3 finish.1
  116.7 13.4 %all_to_all.41.tiles_ref = f32[32,8,128]{2,1,0:T(8,128)S(1)} all-to-all(f32[32,8,128]{2,1,0:T(8,128)S(1)} %finish.1), channel_id=1, replica_groups=mesh['y'=4,'x'=4,'core'=2,'cluster'=8] {'y','x','core'}, dimensions={0} | all-to-all | bytes 262144 | tf_op jit(solution)/shard_map/all_to_all | solution.py:408
  130.1 0.8 place.1
Async XLA Ops:
  88.1 3.4 %collective-permute-start = (f32[128,1024]{1,0:T(8,128)S(1)}, f32[128,1024]{1,0:T(8,128)S(1)}, u32[]{:S(2)}, u32[]{:S(2)}) collective-permute-start(f32[128,1024]{1,0:T(8,128)S(1)} %sums.6), channel_id=1, source_target_pairs={{0,8},{8,0},{1,9},{9,1},{2,10},{10,2},{3,11},{11,3},{4,12},{12,4},... | collective-permute-start | bytes 1572872 | tf_op jit(solution)/shard_map/ppermute | solution.py:361
  92.3 2.7 %collective-permute-start.1 = (f32[256,1024]{1,0:T(8,128)S(1)}, f32[256,1024]{1,0:T(8,128)S(1)}, u32[]{:S(2)}, u32[]{:S(2)}) collective-permute-start(f32[256,1024]{1,0:T(8,128)S(1)} %sums.7), channel_id=1, source_target_pairs={{0,8},{8,0},{1,9},{9,1},{2,10},{10,2},{3,11},{11,3},{4,12},{12,4},... | collective-permute-start | bytes 3145736 | tf_op jit(solution)/shard_map/ppermute | solution.py:361
  92.8 9.9 %collective-permute-start.3 = (f32[128,1024]{1,0:T(8,128)S(1)}, f32[128,1024]{1,0:T(8,128)S(1)}, u32[]{:S(2)}, u32[]{:S(2)}) collective-permute-start(f32[128,1024]{1,0:T(8,128)S(1)} %sums.8), channel_id=1, source_target_pairs={{0,32},{8,136},{16,48},{24,152},{32,0},{40,168},{48,16},{56,184},{... | collective-permute-start | bytes 1572872 | tf_op jit(solution)/shard_map/ppermute | solution.py:373
  95.2 13.1 %collective-permute-start.4 = (f32[128,1024]{1,0:T(8,128)S(1)}, f32[128,1024]{1,0:T(8,128)S(1)}, u32[]{:S(2)}, u32[]{:S(2)}) collective-permute-start(f32[128,1024]{1,0:T(8,128)S(1)} %get-tuple-element.27), channel_id=1, source_target_pairs={{0,16},{8,72},{16,32},{24,88},{32,48},{40,104},{48,0},{56,120},{64... | collective-permute-start | bytes 1572872 | tf_op jit(solution)/shard_map/ppermute | solution.py:373
  96.4 6.2 %collective-permute-start.2 = (f32[128,1024]{1,0:T(8,128)S(1)}, f32[128,1024]{1,0:T(8,128)S(1)}, u32[]{:S(2)}, u32[]{:S(2)}) collective-permute-start(f32[128,1024]{1,0:T(8,128)S(1)} %sums.10), channel_id=1, source_target_pairs={{0,8},{8,0},{1,9},{9,1},{2,10},{10,2},{3,11},{11,3},{4,12},{12,4},... | collective-permute-start | bytes 1572872 | tf_op jit(solution)/shard_map/ppermute | solution.py:361
  97.3 10.9 %collective-permute-start.5 = (f32[128,1024]{1,0:T(8,128)S(1)}, f32[128,1024]{1,0:T(8,128)S(1)}, u32[]{:S(2)}, u32[]{:S(2)}) collective-permute-start(f32[128,1024]{1,0:T(8,128)S(1)} %get-tuple-element.30), channel_id=1, source_target_pairs={{0,48},{8,200},{16,0},{24,216},{32,16},{40,232},{48,32},{56,248},{... | collective-permute-start | bytes 1572872 | tf_op jit(solution)/shard_map/ppermute | solution.py:373
  108.3 5.1 %collective-permute-start.6 = (f32[32,1024]{1,0:T(8,128)S(1)}, f32[32,1024]{1,0:T(8,128)S(1)}, u32[]{:S(2)}, u32[]{:S(2)}) collective-permute-start(f32[32,1024]{1,0:T(8,128)S(1)} %get-tuple-element.32), channel_id=1, source_target_pairs={{0,64},{8,24},{16,80},{24,40},{32,96},{40,56},{48,112},{56,8},{64,... | collective-permute-start | bytes 393224 | tf_op jit(solution)/shard_map/ppermute | solution.py:373
  108.5 6.0 %collective-permute-start.7 = (f32[32,1024]{1,0:T(8,128)S(1)}, f32[32,1024]{1,0:T(8,128)S(1)}, u32[]{:S(2)}, u32[]{:S(2)}) collective-permute-start(f32[32,1024]{1,0:T(8,128)S(1)} %get-tuple-element.33), channel_id=1, source_target_pairs={{0,192},{8,56},{16,208},{24,8},{32,224},{40,24},{48,240},{56,40},{... | collective-permute-start | bytes 393224 | tf_op jit(solution)/shard_map/ppermute | solution.py:373
  111.1 5.3 %collective-permute-start.8 = (f32[32,1024]{1,0:T(8,128)S(1)}, f32[32,1024]{1,0:T(8,128)S(1)}, u32[]{:S(2)}, u32[]{:S(2)}) collective-permute-start(f32[32,1024]{1,0:T(8,128)S(1)} %get-tuple-element.34), channel_id=1, source_target_pairs={{0,128},{8,40},{16,144},{24,56},{32,160},{40,8},{48,176},{56,24},{... | collective-permute-start | bytes 393224 | tf_op jit(solution)/shard_map/ppermute | solution.py:373

commit v5 on v4

--- a/solution.py
+++ b/solution.py
@@ -71,11 +71,21 @@
         rows = pl.ds(start, size)
         return pltpu.make_async_copy(embeddings_ref.at[rows, :], raw_rows.at[rows, :], arrived.at[which])
 
-    fetch_centroids = pltpu.make_async_copy(centroids_ref, raw_centroids, arrived.at[0])
-    fetch_first = fetch(0, chunk, 1)
-    fetch_rest = fetch(chunk, embeddings_ref.shape[0] - chunk, 2)
-    fetch_centroids.start()
+    pieces = 4
+    local = centroids_ref.shape[0]
+    height = local // pieces
+    fetch_centroids = []
+    for piece in range(pieces):
+        rows = pl.ds(piece * height, height)
+        fetch_centroids.append(
+            pltpu.make_async_copy(centroids_ref.at[rows, :], raw_centroids.at[rows, :], arrived.at[piece])
+        )
+    fetch_first = fetch(0, chunk, pieces)
+    fetch_rest = fetch(chunk, embeddings_ref.shape[0] - chunk, pieces + 1)
+    for copy in fetch_centroids:
+        copy.start()
     fetch_first.start()
+    fetch_rest.start()
 
     def normalise(index, out_ref):
         start = pl.multiple_of(index * chunk, chunk)
@@ -97,12 +107,13 @@
             folded = folded + affinity[:, tile * LANES : (tile + 1) * LANES]
         partial[...] += folded
 
-    fetch_centroids.wait()
-    fetch_rest.start()
-    for place, block in enumerate(order):
-        unit_centroids[place * share : (place + 1) * share, :] = unit(
-            raw_centroids[block * share : (block + 1) * share, :]
-        )
+    for piece in range(pieces):
+        fetch_centroids[piece].wait()
+        for place, block in enumerate(order):
+            if block * share // height == piece:
+                unit_centroids[place * share : (place + 1) * share, :] = unit(
+                    raw_centroids[block * share : (block + 1) * share, :]
+                )
     partial[...] = jnp.zeros_like(partial)
     fetch_first.wait()
     normalise(0, even_rows)
@@ -293,7 +304,7 @@
             pltpu.VMEM((local, chunk), f32),
             pltpu.VMEM((local, chunk), f32),
             pltpu.VMEM((local, LANES), f32),
-            pltpu.SemaphoreType.DMA((3,)),
+            pltpu.SemaphoreType.DMA((6,)),
         ],
         compiler_params=params(24),
         name="prepare",
@@ -395,7 +406,7 @@
     second_parts = add(
         functools.partial(fold_kernel, chips_y), "fold", [(share, width)] * chips_y, part_0, own, far, up, down
     )
-    got = [second_parts[0]] + [hop(second_parts[k], k, 1) for k in (1, 3, 2)]
+    got = [second_parts[0]] + [hop(second_parts[k], k, 1) for k in (2, 3, 1)]
     tiles = pl.pallas_call(
         finish_kernel,
         in_specs=[VMEM] * len(got),

time: 131 us -> 130 us (level)
  no operation moved by 1% of the time
where the time goes in v5:
time: 130 us
  blocking collectives  88.8 us (68%)
  Pallas kernels  18.3 us (14%)
  waiting for transfers between devices  14 us (11%)
  starting transfers between devices  8.78 us (7%)
    all_to_all x3, blocking collectives, column_exchange(): return lax.all_to_all(sums, ROWS_DP, 0, 0)  41.2 us
    all_to_all x3, blocking collectives, row_exchange(): return lax.all_to_all(sums, 'cluster', 0, 0)  34.3 us
    ppermute x6, waiting for transfers between devices, hop(): return lax.ppermute(part, ROWS_DP, pairs)  13.7 us
    all_to_all x1, blocking collectives, per_device(): tiles = lax.all_to_all(tiles, ROWS_DP, 0, 0)  13.3 us
    pallas_call x1, Pallas kernels, per_device(): pl.pallas_call(functools.partial(prepare_kernel, order, chunk), in_specs=...  7.45 us
    ppermute x6, starting transfers between devices, hop(): return lax.ppermute(part, ROWS_DP, pairs)  5.48 us
    pallas_call x6, Pallas kernels, weighted(): pl.pallas_call(functools.partial(sums_kernel, (chips_x, chips_y), given,...  5.42 us
    ppermute x3, starting transfers between devices, swap(): return lax.ppermute(part, 'core', ring(2, 1))  3.3 us
  transfers between devices with their start and end apart: 9, of which 7 were waited for; matrix products, arithmetic and copies ran while one was open for 0% of the time, Pallas kernels for 3%

profile of v5, /device:TPU:1, one launch (start us, length us, event | category | flops | bytes accessed | tf_op | source)
XLA Modules:
  0.0 130.0 jit_solution(4367353397497699318)
XLA Ops:
  0.0 7.4 %prepare.1 = (f32[1024,2048]{1,0:T(8,128)S(1)}, bf16[2048,1024]{1,0:T(8,128)(2,1)S(1)}, f32[32,8,128]{2,1,0:T(8,128)S(1)}) custom-call(bf16[2048,1024]{1,0:T(8,128)(2,1)} %embeddings_ref.1, bf16[1024,1024]{1,0:T(8,128)(2,1)} %centroids_ref.1), custom_call_target="tpu_custom_call" | custom-call | tf_op jit(solution)/shard_map/prepare/pallas_call | solution.py:289
  7.5 16.0 %all_to_all.35.columns_ref = f32[32,8,128]{2,1,0:T(8,128)S(1)} all-to-all(f32[32,8,128]{2,1,0:T(8,128)S(1)} %get-tuple-element.20), channel_id=1, replica_groups=mesh['y'=4,'x'=4,'core'=2,'cluster'=8] {'y','x','core'}, dimensions={0} | all-to-all | bytes 262144 | tf_op jit(solution)/shard_map/all_to_all | solution.py:314
  23.5 0.8 rows.3
  24.3 15.2 %all_to_all.36.rows_ref = f32[8,16,128]{2,1,0:T(8,128)S(1)} all-to-all(f32[8,16,128]{2,1,0:T(8,128)S(1)} %rows.3), channel_id=1, replica_groups=mesh['y'=4,'x'=4,'core'=2,'cluster'=8] {'cluster'}, dimensions={0} | all-to-all | bytes 131072 | tf_op jit(solution)/shard_map/all_to_all | solution.py:317
  39.5 0.8 columns.2
  40.3 12.7 %all_to_all.37.columns_ref = f32[32,8,128]{2,1,0:T(8,128)S(1)} all-to-all(f32[32,8,128]{2,1,0:T(8,128)S(1)} %columns.2), channel_id=1, replica_groups=mesh['y'=4,'x'=4,'core'=2,'cluster'=8] {'y','x','core'}, dimensions={0} | all-to-all | bytes 262144 | tf_op jit(solution)/shard_map/all_to_all | solution.py:314
  53.0 0.8 rows.4
  53.9 9.5 %all_to_all.38.rows_ref = f32[8,16,128]{2,1,0:T(8,128)S(1)} all-to-all(f32[8,16,128]{2,1,0:T(8,128)S(1)} %rows.4), channel_id=1, replica_groups=mesh['y'=4,'x'=4,'core'=2,'cluster'=8] {'cluster'}, dimensions={0} | all-to-all | bytes 131072 | tf_op jit(solution)/shard_map/all_to_all | solution.py:317
  63.4 0.8 columns.3
  64.2 12.5 %all_to_all.39.columns_ref = f32[32,8,128]{2,1,0:T(8,128)S(1)} all-to-all(f32[32,8,128]{2,1,0:T(8,128)S(1)} %columns.3), channel_id=1, replica_groups=mesh['y'=4,'x'=4,'core'=2,'cluster'=8] {'y','x','core'}, dimensions={0} | all-to-all | bytes 262144 | tf_op jit(solution)/shard_map/all_to_all | solution.py:314
  76.7 0.8 rows.5
  77.5 9.5 %all_to_all.40.rows_ref = f32[8,16,128]{2,1,0:T(8,128)S(1)} all-to-all(f32[8,16,128]{2,1,0:T(8,128)S(1)} %rows.5), channel_id=1, replica_groups=mesh['y'=4,'x'=4,'core'=2,'cluster'=8] {'cluster'}, dimensions={0} | all-to-all | bytes 131072 | tf_op jit(solution)/shard_map/all_to_all | solution.py:317
  87.1 0.7 sums.6
  87.8 1.9 %collective-permute-start = (f32[128,1024]{1,0:T(8,128)S(1)}, f32[128,1024]{1,0:T(8,128)S(1)}, u32[]{:S(2)}, u32[]{:S(2)}) collective-permute-start(f32[128,1024]{1,0:T(8,128)S(1)} %sums.6), channel_id=1, source_target_pairs={{0,8},{8,0},{1,9},{9,1},{2,10},{10,2},{3,11},{11,3},{4,12},{12,4},... | collective-permute-start | bytes 1572872 | tf_op jit(solution)/shard_map/ppermute | solution.py:372
  89.7 1.3 sums.7
  91.0 0.3 collective-permute-done.rest_0_
  91.2 0.7 sums.8
  92.0 0.5 collective-permute-start.1
  92.4 1.0 collective-permute-start.3
  93.4 1.3 sums.9.own_ref
  94.7 0.1 collective-permute-done.1.other_ref
  94.7 0.1 near.1
  94.8 0.5 collective-permute-start.4
  95.3 0.7 sums.10
  96.1 0.9 collective-permute-start.2
  97.0 1.5 %collective-permute-start.5 = (f32[128,1024]{1,0:T(8,128)S(1)}, f32[128,1024]{1,0:T(8,128)S(1)}, u32[]{:S(2)}, u32[]{:S(2)}) collective-permute-start(f32[128,1024]{1,0:T(8,128)S(1)} %get-tuple-element.30), channel_id=1, source_target_pairs={{0,48},{8,200},{16,0},{24,216},{32,16},{40,232},{48,32},{56,248},{... | collective-permute-start | bytes 1572872 | tf_op jit(solution)/shard_map/ppermute | solution.py:384
  98.5 0.7 sums.11.refs_0_
  99.2 3.1 %collective-permute-done.3.refs_2_ = f32[128,1024]{1,0:T(8,128)S(1)} collective-permute-done((f32[128,1024]{1,0:T(8,128)S(1)}, f32[128,1024]{1,0:T(8,128)S(1)}, u32[]{:S(2)}, u32[]{:S(2)}) %collective-permute-start.3) | collective-permute-done | bytes 524320 | tf_op jit(solution)/shard_map/ppermute | solution.py:384
  102.3 0.0 collective-permute-done.2.refs_1_
  102.3 5.6 %collective-permute-done.4.refs_3_ = f32[128,1024]{1,0:T(8,128)S(1)} collective-permute-done((f32[128,1024]{1,0:T(8,128)S(1)}, f32[128,1024]{1,0:T(8,128)S(1)}, u32[]{:S(2)}, u32[]{:S(2)}) %collective-permute-start.4) | collective-permute-done | bytes 524320 | tf_op jit(solution)/shard_map/ppermute | solution.py:384
  107.9 0.0 collective-permute-done.5.refs_4_
  107.9 0.1 fold.1
  108.0 0.6 collective-permute-start.6
  108.6 1.9 %collective-permute-start.7 = (f32[32,1024]{1,0:T(8,128)S(1)}, f32[32,1024]{1,0:T(8,128)S(1)}, u32[]{:S(2)}, u32[]{:S(2)}) collective-permute-start(f32[32,1024]{1,0:T(8,128)S(1)} %get-tuple-element.33), channel_id=1, source_target_pairs={{0,192},{8,56},{16,208},{24,8},{32,224},{40,24},{48,240},{56,40},{... | collective-permute-start | bytes 393224 | tf_op jit(solution)/shard_map/ppermute | solution.py:384
  110.5 0.0 collective-permute-start.8
  110.5 2.9 %collective-permute-done.6.refs_1_ = f32[32,1024]{1,0:T(8,128)S(1)} collective-permute-done((f32[32,1024]{1,0:T(8,128)S(1)}, f32[32,1024]{1,0:T(8,128)S(1)}, u32[]{:S(2)}, u32[]{:S(2)}) %collective-permute-start.6) | collective-permute-done | bytes 131104 | tf_op jit(solution)/shard_map/ppermute | solution.py:384
  113.4 0.3 collective-permute-done.7.refs_2_
  113.7 1.8 %collective-permute-done.8.refs_3_ = f32[32,1024]{1,0:T(8,128)S(1)} collective-permute-done((f32[32,1024]{1,0:T(8,128)S(1)}, f32[32,1024]{1,0:T(8,128)S(1)}, u32[]{:S(2)}, u32[]{:S(2)}) %collective-permute-start.8) | collective-permute-done | bytes 131104 | tf_op jit(solution)/shard_map/ppermute | solution.py:384
  115.5 0.3 finish.1
  115.8 13.3 %all_to_all.41.tiles_ref = f32[32,8,128]{2,1,0:T(8,128)S(1)} all-to-all(f32[32,8,128]{2,1,0:T(8,128)S(1)} %finish.1), channel_id=1, replica_groups=mesh['y'=4,'x'=4,'core'=2,'cluster'=8] {'y','x','core'}, dimensions={0} | all-to-all | bytes 262144 | tf_op jit(solution)/shard_map/all_to_all | solution.py:419
  129.2 0.8 place.1
Async XLA Ops:
  87.8 3.4 %collective-permute-start = (f32[128,1024]{1,0:T(8,128)S(1)}, f32[128,1024]{1,0:T(8,128)S(1)}, u32[]{:S(2)}, u32[]{:S(2)}) collective-permute-start(f32[128,1024]{1,0:T(8,128)S(1)} %sums.6), channel_id=1, source_target_pairs={{0,8},{8,0},{1,9},{9,1},{2,10},{10,2},{3,11},{11,3},{4,12},{12,4},... | collective-permute-start | bytes 1572872 | tf_op jit(solution)/shard_map/ppermute | solution.py:372
  92.0 2.7 %collective-permute-start.1 = (f32[256,1024]{1,0:T(8,128)S(1)}, f32[256,1024]{1,0:T(8,128)S(1)}, u32[]{:S(2)}, u32[]{:S(2)}) collective-permute-start(f32[256,1024]{1,0:T(8,128)S(1)} %sums.7), channel_id=1, source_target_pairs={{0,8},{8,0},{1,9},{9,1},{2,10},{10,2},{3,11},{11,3},{4,12},{12,4},... | collective-permute-start | bytes 3145736 | tf_op jit(solution)/shard_map/ppermute | solution.py:372
  92.4 9.9 %collective-permute-start.3 = (f32[128,1024]{1,0:T(8,128)S(1)}, f32[128,1024]{1,0:T(8,128)S(1)}, u32[]{:S(2)}, u32[]{:S(2)}) collective-permute-start(f32[128,1024]{1,0:T(8,128)S(1)} %sums.8), channel_id=1, source_target_pairs={{0,32},{8,136},{16,48},{24,152},{32,0},{40,168},{48,16},{56,184},{... | collective-permute-start | bytes 1572872 | tf_op jit(solution)/shard_map/ppermute | solution.py:384
  94.8 13.0 %collective-permute-start.4 = (f32[128,1024]{1,0:T(8,128)S(1)}, f32[128,1024]{1,0:T(8,128)S(1)}, u32[]{:S(2)}, u32[]{:S(2)}) collective-permute-start(f32[128,1024]{1,0:T(8,128)S(1)} %get-tuple-element.27), channel_id=1, source_target_pairs={{0,16},{8,72},{16,32},{24,88},{32,48},{40,104},{48,0},{56,120},{64... | collective-permute-start | bytes 1572872 | tf_op jit(solution)/shard_map/ppermute | solution.py:384
  96.1 6.2 %collective-permute-start.2 = (f32[128,1024]{1,0:T(8,128)S(1)}, f32[128,1024]{1,0:T(8,128)S(1)}, u32[]{:S(2)}, u32[]{:S(2)}) collective-permute-start(f32[128,1024]{1,0:T(8,128)S(1)} %sums.10), channel_id=1, source_target_pairs={{0,8},{8,0},{1,9},{9,1},{2,10},{10,2},{3,11},{11,3},{4,12},{12,4},... | collective-permute-start | bytes 1572872 | tf_op jit(solution)/shard_map/ppermute | solution.py:372
  97.0 10.9 %collective-permute-start.5 = (f32[128,1024]{1,0:T(8,128)S(1)}, f32[128,1024]{1,0:T(8,128)S(1)}, u32[]{:S(2)}, u32[]{:S(2)}) collective-permute-start(f32[128,1024]{1,0:T(8,128)S(1)} %get-tuple-element.30), channel_id=1, source_target_pairs={{0,48},{8,200},{16,0},{24,216},{32,16},{40,232},{48,32},{56,248},{... | collective-permute-start | bytes 1572872 | tf_op jit(solution)/shard_map/ppermute | solution.py:384
  108.0 5.4 %collective-permute-start.6 = (f32[32,1024]{1,0:T(8,128)S(1)}, f32[32,1024]{1,0:T(8,128)S(1)}, u32[]{:S(2)}, u32[]{:S(2)}) collective-permute-start(f32[32,1024]{1,0:T(8,128)S(1)} %get-tuple-element.32), channel_id=1, source_target_pairs={{0,128},{8,40},{16,144},{24,56},{32,160},{40,8},{48,176},{56,24},{... | collective-permute-start | bytes 393224 | tf_op jit(solution)/shard_map/ppermute | solution.py:384
  108.6 5.1 %collective-permute-start.7 = (f32[32,1024]{1,0:T(8,128)S(1)}, f32[32,1024]{1,0:T(8,128)S(1)}, u32[]{:S(2)}, u32[]{:S(2)}) collective-permute-start(f32[32,1024]{1,0:T(8,128)S(1)} %get-tuple-element.33), channel_id=1, source_target_pairs={{0,192},{8,56},{16,208},{24,8},{32,224},{40,24},{48,240},{56,40},{... | collective-permute-start | bytes 393224 | tf_op jit(solution)/shard_map/ppermute | solution.py:384
  110.5 5.0 %collective-permute-start.8 = (f32[32,1024]{1,0:T(8,128)S(1)}, f32[32,1024]{1,0:T(8,128)S(1)}, u32[]{:S(2)}, u32[]{:S(2)}) collective-permute-start(f32[32,1024]{1,0:T(8,128)S(1)} %get-tuple-element.34), channel_id=1, source_target_pairs={{0,64},{8,24},{16,80},{24,40},{32,96},{40,56},{48,112},{56,8},{64,... | collective-permute-start | bytes 393224 | tf_op jit(solution)/shard_map/ppermute | solution.py:384

commit v6 on v5

--- a/solution.py
+++ b/solution.py
@@ -194,24 +194,25 @@
         ).astype(jnp.bfloat16)
 
 
-def sums_kernel(counts, given, distances, rows_ref, kernel_ref, unit_ref, *rest):
-    received, (out_ref, weight_scratch) = rest[:-2], rest[-2:]
+def sums_kernel(counts, blocks, rows_ref, kernel_ref, unit_ref, *rest):
+    outs, weight_scratch = rest[:-1], rest[-1]
     slow, fast = counts
     half = slow * fast
     share = kernel_ref.shape[0] // (2 * half)
     scale = 1.0 / jnp.sum(rows_ref[...], axis=0)
     y, x, core = (lax.axis_index(name) for name in ROWS_DP)
-    base = 1 - core if given else core
-    first, second = jnp.where(base == 0, x, y), jnp.where(base == 0, y, x)
-    for part, a in enumerate(distances):
+    for part, (other, a) in enumerate(blocks):
+        base = 1 - core if other else core
+        first, second = jnp.where(base == 0, x, y), jnp.where(base == 0, y, x)
         for b in range(fast):
             block = base * half + lax.rem(first + a, slow) * fast + lax.rem(second + b, fast)
             weigh(kernel_ref, scale, weight_scratch, pl.multiple_of(block * share, share), part * fast + b, share)
-    height = 128
-    for part in range(weight_scratch.shape[0] // height):
-        rows = slice(part * height, (part + 1) * height)
-        sums = jnp.dot(weight_scratch[rows, :], unit_ref[...], preferred_element_type=jnp.float32)
-        out_ref[rows, :] = sums + received[0][rows, :] if received else sums
+    height = fast * share
+    sums = jnp.dot(weight_scratch[...], unit_ref[...], preferred_element_type=jnp.float32)
+    start = 0
+    for out_ref in outs:
+        out_ref[...] = sums[start : start + out_ref.shape[0], :]
+        start += out_ref.shape[0]
 
 
 def add_kernel(own_ref, other_ref, *outs):
@@ -341,13 +342,14 @@
 
     height = chips_y * share
 
-    def weighted(row_sums, given, distances, *received):
-        count = len(distances)
+    def weighted(row_sums, *groups):
+        blocks = [block for group in groups for block in group]
+        count = len(blocks)
         return pl.pallas_call(
-            functools.partial(sums_kernel, (chips_x, chips_y), given, distances),
-            in_specs=[VMEM] * (3 + len(received)),
-            out_specs=VMEM,
-            out_shape=pltpu.VMEM((count * height, width), f32),
+            functools.partial(sums_kernel, (chips_x, chips_y), blocks),
+            in_specs=[VMEM] * 3,
+            out_specs=[VMEM] * len(groups),
+            out_shape=[pltpu.VMEM((len(group) * height, width), f32) for group in groups],
             scratch_shapes=[pltpu.VMEM((count * height, rows), bf16)],
             compiler_params=params(6),
             cost_estimate=pl.CostEstimate(
@@ -356,7 +358,7 @@
                 transcendentals=0,
             ),
             name="sums",
-        )(resident(row_sums), resident(kernel), resident(unit_rows), *[resident(part) for part in received])
+        )(resident(row_sums), resident(kernel), resident(unit_rows))
 
     def add(body, name, shapes, *arrays):
         return pl.pallas_call(
@@ -386,23 +388,19 @@
     def after(value, *others):
         return lax.optimization_barrier((value,) + others)[0]
 
-    far = weighted(row_sums, True, (2,))
+    far, far_own = weighted(row_sums, [(1, 2)], [(0, 2)])
     row_sums = after(row_sums, far)
     far = swap(far)
-    near = weighted(row_sums, True, (1, 3))
-    row_sums = after(row_sums, near)
-    far = weighted(row_sums, False, (2,), far)
-    near = swap(after(near, far))
-    row_sums = after(row_sums, far)
+    (near,) = weighted(row_sums, [(1, 1), (1, 3)])
+    (far,) = add(add_kernel, "far", [(height, width)], after(far_own, near), far)
+    near, row_sums = swap(after(near, far)), after(row_sums, far)
     far = hop(far, 2, 0)
-    near_own = weighted(row_sums, False, (1, 3))
+    (near_own,) = weighted(row_sums, [(0, 1), (0, 3)])
     up, down = add(add_kernel, "near", [(height, width)] * 2, near_own, near)
     row_sums = after(row_sums, up)
     up, down = hop(up, 1, 0), hop(down, 3, 0)
-    own = weighted(row_sums, True, (0,))
-    row_sums = after(row_sums, own)
+    own, part_0 = weighted(row_sums, [(1, 0)], [(0, 0)])
     own = swap(own)
-    part_0 = weighted(row_sums, False, (0,))
     second_parts = add(
         functools.partial(fold_kernel, chips_y), "fold", [(share, width)] * chips_y, part_0, own, far, up, down
     )

time: 130 us -> 130 us (level)
    pallas_call x6 -> x4, Pallas kernels: 5.42 us -> 5.03 us  [weighted(): pl.pallas_call(functools.partial(sums_kernel, (chips_x, chips_y), blocks)...]
where the time goes in v6:
time: 130 us
  blocking collectives  88.8 us (68%)
  Pallas kernels  18 us (14%)
  waiting for transfers between devices  14.2 us (11%)
  starting transfers between devices  8.8 us (7%)
    all_to_all x3, blocking collectives, column_exchange(): return lax.all_to_all(sums, ROWS_DP, 0, 0)  41.2 us
    all_to_all x3, blocking collectives, row_exchange(): return lax.all_to_all(sums, 'cluster', 0, 0)  34.3 us
    ppermute x6, waiting for transfers between devices, hop(): return lax.ppermute(part, ROWS_DP, pairs)  13.9 us
    all_to_all x1, blocking collectives, per_device(): tiles = lax.all_to_all(tiles, ROWS_DP, 0, 0)  13.3 us
    pallas_call x1, Pallas kernels, per_device(): pl.pallas_call(functools.partial(prepare_kernel, order, chunk), in_specs=...  7.45 us
    ppermute x6, starting transfers between devices, hop(): return lax.ppermute(part, ROWS_DP, pairs)  5.47 us
    pallas_call x4, Pallas kernels, weighted(): pl.pallas_call(functools.partial(sums_kernel, (chips_x, chips_y), blocks)...  5.03 us
    ppermute x3, starting transfers between devices, swap(): return lax.ppermute(part, 'core', ring(2, 1))  3.33 us
  transfers between devices with their start and end apart: 9, of which 7 were waited for; matrix products, arithmetic and copies ran while one was open for 0% of the time, Pallas kernels for 3%

profile of v6, /device:TPU:1, one launch (start us, length us, event | category | flops | bytes accessed | tf_op | source)
XLA Modules:
  0.0 129.9 jit_solution(700198780680840526)
XLA Ops:
  0.0 7.4 %prepare.1 = (f32[1024,2048]{1,0:T(8,128)S(1)}, bf16[2048,1024]{1,0:T(8,128)(2,1)S(1)}, f32[32,8,128]{2,1,0:T(8,128)S(1)}) custom-call(bf16[2048,1024]{1,0:T(8,128)(2,1)} %embeddings_ref.1, bf16[1024,1024]{1,0:T(8,128)(2,1)} %centroids_ref.1), custom_call_target="tpu_custom_call" | custom-call | tf_op jit(solution)/shard_map/prepare/pallas_call | solution.py:290
  7.5 16.0 %all_to_all.35.columns_ref = f32[32,8,128]{2,1,0:T(8,128)S(1)} all-to-all(f32[32,8,128]{2,1,0:T(8,128)S(1)} %get-tuple-element.23), channel_id=1, replica_groups=mesh['y'=4,'x'=4,'core'=2,'cluster'=8] {'y','x','core'}, dimensions={0} | all-to-all | bytes 262144 | tf_op jit(solution)/shard_map/all_to_all | solution.py:315
  23.5 0.8 rows.3
  24.3 15.2 %all_to_all.36.rows_ref = f32[8,16,128]{2,1,0:T(8,128)S(1)} all-to-all(f32[8,16,128]{2,1,0:T(8,128)S(1)} %rows.3), channel_id=1, replica_groups=mesh['y'=4,'x'=4,'core'=2,'cluster'=8] {'cluster'}, dimensions={0} | all-to-all | bytes 131072 | tf_op jit(solution)/shard_map/all_to_all | solution.py:318
  39.5 0.8 columns.2
  40.3 12.7 %all_to_all.37.columns_ref = f32[32,8,128]{2,1,0:T(8,128)S(1)} all-to-all(f32[32,8,128]{2,1,0:T(8,128)S(1)} %columns.2), channel_id=1, replica_groups=mesh['y'=4,'x'=4,'core'=2,'cluster'=8] {'y','x','core'}, dimensions={0} | all-to-all | bytes 262144 | tf_op jit(solution)/shard_map/all_to_all | solution.py:315
  53.0 0.8 rows.4
  53.9 9.5 %all_to_all.38.rows_ref = f32[8,16,128]{2,1,0:T(8,128)S(1)} all-to-all(f32[8,16,128]{2,1,0:T(8,128)S(1)} %rows.4), channel_id=1, replica_groups=mesh['y'=4,'x'=4,'core'=2,'cluster'=8] {'cluster'}, dimensions={0} | all-to-all | bytes 131072 | tf_op jit(solution)/shard_map/all_to_all | solution.py:318
  63.4 0.8 columns.3
  64.2 12.5 %all_to_all.39.columns_ref = f32[32,8,128]{2,1,0:T(8,128)S(1)} all-to-all(f32[32,8,128]{2,1,0:T(8,128)S(1)} %columns.3), channel_id=1, replica_groups=mesh['y'=4,'x'=4,'core'=2,'cluster'=8] {'y','x','core'}, dimensions={0} | all-to-all | bytes 262144 | tf_op jit(solution)/shard_map/all_to_all | solution.py:315
  76.7 0.8 rows.5
  77.5 9.5 %all_to_all.40.rows_ref = f32[8,16,128]{2,1,0:T(8,128)S(1)} all-to-all(f32[8,16,128]{2,1,0:T(8,128)S(1)} %rows.5), channel_id=1, replica_groups=mesh['y'=4,'x'=4,'core'=2,'cluster'=8] {'cluster'}, dimensions={0} | all-to-all | bytes 131072 | tf_op jit(solution)/shard_map/all_to_all | solution.py:318
  87.1 1.2 sums.4
  88.3 1.7 %collective-permute-start = (f32[128,1024]{1,0:T(8,128)S(1)}, f32[128,1024]{1,0:T(8,128)S(1)}, u32[]{:S(2)}, u32[]{:S(2)}) collective-permute-start(f32[128,1024]{1,0:T(8,128)S(1)} %get-tuple-element.26), channel_id=1, source_target_pairs={{0,8},{8,0},{1,9},{9,1},{2,10},{10,2},{3,11},{11,3},{4,12},{12,4},... | collective-permute-start | bytes 1572872 | tf_op jit(solution)/shard_map/ppermute | solution.py:374
  90.1 1.3 sums.5
  91.3 0.3 collective-permute-done.other_ref
  91.6 0.1 far.1
  91.6 0.6 collective-permute-start.1
  92.3 1.0 collective-permute-start.3
  93.3 1.3 sums.6.own_ref
  94.5 0.1 collective-permute-done.1.other_ref
  94.6 0.1 near.1
  94.7 0.5 collective-permute-start.4
  95.2 1.3 sums.7
  96.5 0.9 collective-permute-start.2
  97.4 1.5 %collective-permute-start.5 = (f32[128,1024]{1,0:T(8,128)S(1)}, f32[128,1024]{1,0:T(8,128)S(1)}, u32[]{:S(2)}, u32[]{:S(2)}) collective-permute-start(f32[128,1024]{1,0:T(8,128)S(1)} %get-tuple-element.36), channel_id=1, source_target_pairs={{0,48},{8,200},{16,0},{24,216},{32,16},{40,232},{48,32},{56,248},{... | collective-permute-start | bytes 1572872 | tf_op jit(solution)/shard_map/ppermute | solution.py:386
  98.9 3.3 %collective-permute-done.3.refs_2_ = f32[128,1024]{1,0:T(8,128)S(1)} collective-permute-done((f32[128,1024]{1,0:T(8,128)S(1)}, f32[128,1024]{1,0:T(8,128)S(1)}, u32[]{:S(2)}, u32[]{:S(2)}) %collective-permute-start.3) | collective-permute-done | bytes 524320 | tf_op jit(solution)/shard_map/ppermute | solution.py:386
  102.2 0.0 collective-permute-done.2.refs_1_
  102.2 5.6 %collective-permute-done.4.refs_3_ = f32[128,1024]{1,0:T(8,128)S(1)} collective-permute-done((f32[128,1024]{1,0:T(8,128)S(1)}, f32[128,1024]{1,0:T(8,128)S(1)}, u32[]{:S(2)}, u32[]{:S(2)}) %collective-permute-start.4) | collective-permute-done | bytes 524320 | tf_op jit(solution)/shard_map/ppermute | solution.py:386
  107.7 0.0 collective-permute-done.5.refs_4_
  107.7 0.1 fold.1
  107.9 0.6 collective-permute-start.6
  108.4 1.9 %collective-permute-start.7 = (f32[32,1024]{1,0:T(8,128)S(1)}, f32[32,1024]{1,0:T(8,128)S(1)}, u32[]{:S(2)}, u32[]{:S(2)}) collective-permute-start(f32[32,1024]{1,0:T(8,128)S(1)} %get-tuple-element.39), channel_id=1, source_target_pairs={{0,192},{8,56},{16,208},{24,8},{32,224},{40,24},{48,240},{56,40},{... | collective-permute-start | bytes 393224 | tf_op jit(solution)/shard_map/ppermute | solution.py:386
  110.4 0.0 collective-permute-start.8
  110.4 2.9 %collective-permute-done.6.refs_1_ = f32[32,1024]{1,0:T(8,128)S(1)} collective-permute-done((f32[32,1024]{1,0:T(8,128)S(1)}, f32[32,1024]{1,0:T(8,128)S(1)}, u32[]{:S(2)}, u32[]{:S(2)}) %collective-permute-start.6) | collective-permute-done | bytes 131104 | tf_op jit(solution)/shard_map/ppermute | solution.py:386
  113.3 0.3 collective-permute-done.7.refs_2_
  113.6 1.8 %collective-permute-done.8.refs_3_ = f32[32,1024]{1,0:T(8,128)S(1)} collective-permute-done((f32[32,1024]{1,0:T(8,128)S(1)}, f32[32,1024]{1,0:T(8,128)S(1)}, u32[]{:S(2)}, u32[]{:S(2)}) %collective-permute-start.8) | collective-permute-done | bytes 131104 | tf_op jit(solution)/shard_map/ppermute | solution.py:386
  115.4 0.3 finish.1
  115.7 13.3 %all_to_all.41.tiles_ref = f32[32,8,128]{2,1,0:T(8,128)S(1)} all-to-all(f32[32,8,128]{2,1,0:T(8,128)S(1)} %finish.1), channel_id=1, replica_groups=mesh['y'=4,'x'=4,'core'=2,'cluster'=8] {'y','x','core'}, dimensions={0} | all-to-all | bytes 262144 | tf_op jit(solution)/shard_map/all_to_all | solution.py:417
  129.1 0.8 place.1
Async XLA Ops:
  88.3 3.3 %collective-permute-start = (f32[128,1024]{1,0:T(8,128)S(1)}, f32[128,1024]{1,0:T(8,128)S(1)}, u32[]{:S(2)}, u32[]{:S(2)}) collective-permute-start(f32[128,1024]{1,0:T(8,128)S(1)} %get-tuple-element.26), channel_id=1, source_target_pairs={{0,8},{8,0},{1,9},{9,1},{2,10},{10,2},{3,11},{11,3},{4,12},{12,4},... | collective-permute-start | bytes 1572872 | tf_op jit(solution)/shard_map/ppermute | solution.py:374
  91.6 2.9 %collective-permute-start.1 = (f32[256,1024]{1,0:T(8,128)S(1)}, f32[256,1024]{1,0:T(8,128)S(1)}, u32[]{:S(2)}, u32[]{:S(2)}) collective-permute-start(f32[256,1024]{1,0:T(8,128)S(1)} %sums.5), channel_id=1, source_target_pairs={{0,8},{8,0},{1,9},{9,1},{2,10},{10,2},{3,11},{11,3},{4,12},{12,4},... | collective-permute-start | bytes 3145736 | tf_op jit(solution)/shard_map/ppermute | solution.py:374
  92.3 9.9 %collective-permute-start.3 = (f32[128,1024]{1,0:T(8,128)S(1)}, f32[128,1024]{1,0:T(8,128)S(1)}, u32[]{:S(2)}, u32[]{:S(2)}) collective-permute-start(f32[128,1024]{1,0:T(8,128)S(1)} %far.1), channel_id=1, source_target_pairs={{0,32},{8,136},{16,48},{24,152},{32,0},{40,168},{48,16},{56,184},{... | collective-permute-start | bytes 1572872 | tf_op jit(solution)/shard_map/ppermute | solution.py:386
  94.7 13.1 %collective-permute-start.4 = (f32[128,1024]{1,0:T(8,128)S(1)}, f32[128,1024]{1,0:T(8,128)S(1)}, u32[]{:S(2)}, u32[]{:S(2)}) collective-permute-start(f32[128,1024]{1,0:T(8,128)S(1)} %get-tuple-element.32), channel_id=1, source_target_pairs={{0,16},{8,72},{16,32},{24,88},{32,48},{40,104},{48,0},{56,120},{64... | collective-permute-start | bytes 1572872 | tf_op jit(solution)/shard_map/ppermute | solution.py:386
  96.5 5.7 %collective-permute-start.2 = (f32[128,1024]{1,0:T(8,128)S(1)}, f32[128,1024]{1,0:T(8,128)S(1)}, u32[]{:S(2)}, u32[]{:S(2)}) collective-permute-start(f32[128,1024]{1,0:T(8,128)S(1)} %get-tuple-element.35), channel_id=1, source_target_pairs={{0,8},{8,0},{1,9},{9,1},{2,10},{10,2},{3,11},{11,3},{4,12},{12,4},... | collective-permute-start | bytes 1572872 | tf_op jit(solution)/shard_map/ppermute | solution.py:374
  97.4 10.3 %collective-permute-start.5 = (f32[128,1024]{1,0:T(8,128)S(1)}, f32[128,1024]{1,0:T(8,128)S(1)}, u32[]{:S(2)}, u32[]{:S(2)}) collective-permute-start(f32[128,1024]{1,0:T(8,128)S(1)} %get-tuple-element.36), channel_id=1, source_target_pairs={{0,48},{8,200},{16,0},{24,216},{32,16},{40,232},{48,32},{56,248},{... | collective-permute-start | bytes 1572872 | tf_op jit(solution)/shard_map/ppermute | solution.py:386
  107.9 5.4 %collective-permute-start.6 = (f32[32,1024]{1,0:T(8,128)S(1)}, f32[32,1024]{1,0:T(8,128)S(1)}, u32[]{:S(2)}, u32[]{:S(2)}) collective-permute-start(f32[32,1024]{1,0:T(8,128)S(1)} %get-tuple-element.38), channel_id=1, source_target_pairs={{0,128},{8,40},{16,144},{24,56},{32,160},{40,8},{48,176},{56,24},{... | collective-permute-start | bytes 393224 | tf_op jit(solution)/shard_map/ppermute | solution.py:386
  108.4 5.1 %collective-permute-start.7 = (f32[32,1024]{1,0:T(8,128)S(1)}, f32[32,1024]{1,0:T(8,128)S(1)}, u32[]{:S(2)}, u32[]{:S(2)}) collective-permute-start(f32[32,1024]{1,0:T(8,128)S(1)} %get-tuple-element.39), channel_id=1, source_target_pairs={{0,192},{8,56},{16,208},{24,8},{32,224},{40,24},{48,240},{56,40},{... | collective-permute-start | bytes 393224 | tf_op jit(solution)/shard_map/ppermute | solution.py:386
  110.4 5.0 %collective-permute-start.8 = (f32[32,1024]{1,0:T(8,128)S(1)}, f32[32,1024]{1,0:T(8,128)S(1)}, u32[]{:S(2)}, u32[]{:S(2)}) collective-permute-start(f32[32,1024]{1,0:T(8,128)S(1)} %get-tuple-element.40), channel_id=1, source_target_pairs={{0,64},{8,24},{16,80},{24,40},{32,96},{40,56},{48,112},{56,8},{64,... | collective-permute-start | bytes 393224 | tf_op jit(solution)/shard_map/ppermute | solution.py:386

commit v7 on v5

--- a/solution.py
+++ b/solution.py
@@ -40,11 +40,11 @@
 
 def share_order(chips_y, chips_x, share):
     order = []
+    for y in range(chips_y):
+        for x in range(chips_x):
+            order.append((chips_x * y + x) * 2)
     for x in range(chips_x):
         for y in range(chips_y):
-            order.append((chips_x * y + x) * 2)
-    for y in range(chips_y):
-        for x in range(chips_x):
             order.append((chips_x * y + x) * 2 + 1)
     return order
 
@@ -202,7 +202,7 @@
     scale = 1.0 / jnp.sum(rows_ref[...], axis=0)
     y, x, core = (lax.axis_index(name) for name in ROWS_DP)
     base = 1 - core if given else core
-    first, second = jnp.where(base == 0, x, y), jnp.where(base == 0, y, x)
+    first, second = jnp.where(base == 0, y, x), jnp.where(base == 0, x, y)
     for part, a in enumerate(distances):
         for b in range(fast):
             block = base * half + lax.rem(first + a, slow) * fast + lax.rem(second + b, fast)
@@ -394,11 +394,11 @@
     far = weighted(row_sums, False, (2,), far)
     near = swap(after(near, far))
     row_sums = after(row_sums, far)
-    far = hop(far, 2, 0)
+    far = hop(far, 2, 1)
     near_own = weighted(row_sums, False, (1, 3))
     up, down = add(add_kernel, "near", [(height, width)] * 2, near_own, near)
     row_sums = after(row_sums, up)
-    up, down = hop(up, 1, 0), hop(down, 3, 0)
+    up, down = hop(up, 1, 1), hop(down, 3, 1)
     own = weighted(row_sums, True, (0,))
     row_sums = after(row_sums, own)
     own = swap(own)
@@ -406,7 +406,7 @@
     second_parts = add(
         functools.partial(fold_kernel, chips_y), "fold", [(share, width)] * chips_y, part_0, own, far, up, down
     )
-    got = [second_parts[0]] + [hop(second_parts[k], k, 1) for k in (2, 3, 1)]
+    got = [second_parts[0]] + [hop(second_parts[k], k, 0) for k in (2, 3, 1)]
     tiles = pl.pallas_call(
         finish_kernel,
         in_specs=[VMEM] * len(got),

time: 130 us -> 130 us (level)
  transfers between devices with their start and end apart: 9 -> 9, of which waited for: 7 -> 6; matrix products, arithmetic and copies ran while one was open for 0% -> 0% of each run, Pallas kernels for 3% -> 3%
where the time goes in v7:
time: 130 us
  blocking collectives  88.8 us (68%)
  Pallas kernels  18.3 us (14%)
  waiting for transfers between devices  14.2 us (11%)
  starting transfers between devices  8.59 us (7%)
    all_to_all x3, blocking collectives, column_exchange(): return lax.all_to_all(sums, ROWS_DP, 0, 0)  41.2 us
    all_to_all x3, blocking collectives, row_exchange(): return lax.all_to_all(sums, 'cluster', 0, 0)  34.2 us
    ppermute x6, waiting for transfers between devices, hop(): return lax.ppermute(part, ROWS_DP, pairs)  13.7 us
    all_to_all x1, blocking collectives, per_device(): tiles = lax.all_to_all(tiles, ROWS_DP, 0, 0)  13.4 us
    pallas_call x1, Pallas kernels, per_device(): pl.pallas_call(functools.partial(prepare_kernel, order, chunk), in_specs=...  7.46 us
    ppermute x6, starting transfers between devices, hop(): return lax.ppermute(part, ROWS_DP, pairs)  5.6 us
    pallas_call x6, Pallas kernels, weighted(): pl.pallas_call(functools.partial(sums_kernel, (chips_x, chips_y), given,...  5.42 us
    ppermute x3, starting transfers between devices, swap(): return lax.ppermute(part, 'core', ring(2, 1))  2.98 us
  transfers between devices with their start and end apart: 9, of which 6 were waited for; matrix products, arithmetic and copies ran while one was open for 0% of the time, Pallas kernels for 3%

profile of v7, /device:TPU:1, one launch (start us, length us, event | category | flops | bytes accessed | tf_op | source)
XLA Modules:
  0.0 130.0 jit_solution(16994144683034206985)
XLA Ops:
  0.0 7.5 %prepare.1 = (f32[1024,2048]{1,0:T(8,128)S(1)}, bf16[2048,1024]{1,0:T(8,128)(2,1)S(1)}, f32[32,8,128]{2,1,0:T(8,128)S(1)}) custom-call(bf16[2048,1024]{1,0:T(8,128)(2,1)} %embeddings_ref.1, bf16[1024,1024]{1,0:T(8,128)(2,1)} %centroids_ref.1), custom_call_target="tpu_custom_call" | custom-call | tf_op jit(solution)/shard_map/prepare/pallas_call | solution.py:289
  7.5 16.0 %all_to_all.35.columns_ref = f32[32,8,128]{2,1,0:T(8,128)S(1)} all-to-all(f32[32,8,128]{2,1,0:T(8,128)S(1)} %get-tuple-element.20), channel_id=1, replica_groups=mesh['y'=4,'x'=4,'core'=2,'cluster'=8] {'y','x','core'}, dimensions={0} | all-to-all | bytes 262144 | tf_op jit(solution)/shard_map/all_to_all | solution.py:314
  23.5 0.8 rows.3
  24.3 15.2 %all_to_all.36.rows_ref = f32[8,16,128]{2,1,0:T(8,128)S(1)} all-to-all(f32[8,16,128]{2,1,0:T(8,128)S(1)} %rows.3), channel_id=1, replica_groups=mesh['y'=4,'x'=4,'core'=2,'cluster'=8] {'cluster'}, dimensions={0} | all-to-all | bytes 131072 | tf_op jit(solution)/shard_map/all_to_all | solution.py:317
  39.5 0.8 columns.2
  40.3 12.7 %all_to_all.37.columns_ref = f32[32,8,128]{2,1,0:T(8,128)S(1)} all-to-all(f32[32,8,128]{2,1,0:T(8,128)S(1)} %columns.2), channel_id=1, replica_groups=mesh['y'=4,'x'=4,'core'=2,'cluster'=8] {'y','x','core'}, dimensions={0} | all-to-all | bytes 262144 | tf_op jit(solution)/shard_map/all_to_all | solution.py:314
  53.0 0.8 rows.4
  53.9 9.5 %all_to_all.38.rows_ref = f32[8,16,128]{2,1,0:T(8,128)S(1)} all-to-all(f32[8,16,128]{2,1,0:T(8,128)S(1)} %rows.4), channel_id=1, replica_groups=mesh['y'=4,'x'=4,'core'=2,'cluster'=8] {'cluster'}, dimensions={0} | all-to-all | bytes 131072 | tf_op jit(solution)/shard_map/all_to_all | solution.py:317
  63.4 0.8 columns.3
  64.2 12.5 %all_to_all.39.columns_ref = f32[32,8,128]{2,1,0:T(8,128)S(1)} all-to-all(f32[32,8,128]{2,1,0:T(8,128)S(1)} %columns.3), channel_id=1, replica_groups=mesh['y'=4,'x'=4,'core'=2,'cluster'=8] {'y','x','core'}, dimensions={0} | all-to-all | bytes 262144 | tf_op jit(solution)/shard_map/all_to_all | solution.py:314
  76.7 0.8 rows.5
  77.5 9.5 %all_to_all.40.rows_ref = f32[8,16,128]{2,1,0:T(8,128)S(1)} all-to-all(f32[8,16,128]{2,1,0:T(8,128)S(1)} %rows.5), channel_id=1, replica_groups=mesh['y'=4,'x'=4,'core'=2,'cluster'=8] {'cluster'}, dimensions={0} | all-to-all | bytes 131072 | tf_op jit(solution)/shard_map/all_to_all | solution.py:317
  87.1 0.7 sums.6
  87.8 1.9 %collective-permute-start = (f32[128,1024]{1,0:T(8,128)S(1)}, f32[128,1024]{1,0:T(8,128)S(1)}, u32[]{:S(2)}, u32[]{:S(2)}) collective-permute-start(f32[128,1024]{1,0:T(8,128)S(1)} %sums.6), channel_id=1, source_target_pairs={{0,8},{8,0},{1,9},{9,1},{2,10},{10,2},{3,11},{11,3},{4,12},{12,4},... | collective-permute-start | bytes 1572872 | tf_op jit(solution)/shard_map/ppermute | solution.py:372
  89.7 1.3 sums.7
  91.0 0.3 collective-permute-done.rest_0_
  91.2 0.7 sums.8
  92.0 0.5 collective-permute-start.1
  92.4 0.8 collective-permute-start.3
  93.2 1.3 sums.9.own_ref
  94.5 0.2 collective-permute-done.1.other_ref
  94.7 0.1 near.1
  94.8 0.7 collective-permute-start.4
  95.5 0.7 sums.10
  96.2 0.6 collective-permute-start.2
  96.8 1.7 %collective-permute-start.5 = (f32[128,1024]{1,0:T(8,128)S(1)}, f32[128,1024]{1,0:T(8,128)S(1)}, u32[]{:S(2)}, u32[]{:S(2)}) collective-permute-start(f32[128,1024]{1,0:T(8,128)S(1)} %get-tuple-element.30), channel_id=1, source_target_pairs={{0,192},{8,56},{16,208},{24,8},{32,224},{40,24},{48,240},{56,40},{... | collective-permute-start | bytes 1572872 | tf_op jit(solution)/shard_map/ppermute | solution.py:384
  98.5 0.7 sums.11.refs_0_
  99.2 3.1 %collective-permute-done.3.refs_2_ = f32[128,1024]{1,0:T(8,128)S(1)} collective-permute-done((f32[128,1024]{1,0:T(8,128)S(1)}, f32[128,1024]{1,0:T(8,128)S(1)}, u32[]{:S(2)}, u32[]{:S(2)}) %collective-permute-start.3) | collective-permute-done | bytes 524320 | tf_op jit(solution)/shard_map/ppermute | solution.py:384
  102.3 0.0 collective-permute-done.2.refs_1_
  102.3 5.6 %collective-permute-done.4.refs_3_ = f32[128,1024]{1,0:T(8,128)S(1)} collective-permute-done((f32[128,1024]{1,0:T(8,128)S(1)}, f32[128,1024]{1,0:T(8,128)S(1)}, u32[]{:S(2)}, u32[]{:S(2)}) %collective-permute-start.4) | collective-permute-done | bytes 524320 | tf_op jit(solution)/shard_map/ppermute | solution.py:384
  107.9 0.0 collective-permute-done.5.refs_4_
  107.9 0.1 fold.1
  108.0 0.8 collective-permute-start.6
  108.8 1.7 %collective-permute-start.7 = (f32[32,1024]{1,0:T(8,128)S(1)}, f32[32,1024]{1,0:T(8,128)S(1)}, u32[]{:S(2)}, u32[]{:S(2)}) collective-permute-start(f32[32,1024]{1,0:T(8,128)S(1)} %get-tuple-element.33), channel_id=1, source_target_pairs={{0,48},{8,200},{16,0},{24,216},{32,16},{40,232},{48,32},{56,248},{... | collective-permute-start | bytes 393224 | tf_op jit(solution)/shard_map/ppermute | solution.py:384
  110.5 0.0 collective-permute-start.8
  110.5 2.9 %collective-permute-done.6.refs_1_ = f32[32,1024]{1,0:T(8,128)S(1)} collective-permute-done((f32[32,1024]{1,0:T(8,128)S(1)}, f32[32,1024]{1,0:T(8,128)S(1)}, u32[]{:S(2)}, u32[]{:S(2)}) %collective-permute-start.6) | collective-permute-done | bytes 131104 | tf_op jit(solution)/shard_map/ppermute | solution.py:384
  113.4 0.0 collective-permute-done.7.refs_2_
  113.4 2.1 %collective-permute-done.8.refs_3_ = f32[32,1024]{1,0:T(8,128)S(1)} collective-permute-done((f32[32,1024]{1,0:T(8,128)S(1)}, f32[32,1024]{1,0:T(8,128)S(1)}, u32[]{:S(2)}, u32[]{:S(2)}) %collective-permute-start.8) | collective-permute-done | bytes 131104 | tf_op jit(solution)/shard_map/ppermute | solution.py:384
  115.5 0.3 finish.1
  115.8 13.4 %all_to_all.41.tiles_ref = f32[32,8,128]{2,1,0:T(8,128)S(1)} all-to-all(f32[32,8,128]{2,1,0:T(8,128)S(1)} %finish.1), channel_id=1, replica_groups=mesh['y'=4,'x'=4,'core'=2,'cluster'=8] {'y','x','core'}, dimensions={0} | all-to-all | bytes 262144 | tf_op jit(solution)/shard_map/all_to_all | solution.py:419
  129.2 0.8 place.1
Async XLA Ops:
  87.8 3.4 %collective-permute-start = (f32[128,1024]{1,0:T(8,128)S(1)}, f32[128,1024]{1,0:T(8,128)S(1)}, u32[]{:S(2)}, u32[]{:S(2)}) collective-permute-start(f32[128,1024]{1,0:T(8,128)S(1)} %sums.6), channel_id=1, source_target_pairs={{0,8},{8,0},{1,9},{9,1},{2,10},{10,2},{3,11},{11,3},{4,12},{12,4},... | collective-permute-start | bytes 1572872 | tf_op jit(solution)/shard_map/ppermute | solution.py:372
  92.0 2.8 %collective-permute-start.1 = (f32[256,1024]{1,0:T(8,128)S(1)}, f32[256,1024]{1,0:T(8,128)S(1)}, u32[]{:S(2)}, u32[]{:S(2)}) collective-permute-start(f32[256,1024]{1,0:T(8,128)S(1)} %sums.7), channel_id=1, source_target_pairs={{0,8},{8,0},{1,9},{9,1},{2,10},{10,2},{3,11},{11,3},{4,12},{12,4},... | collective-permute-start | bytes 3145736 | tf_op jit(solution)/shard_map/ppermute | solution.py:372
  92.4 9.9 %collective-permute-start.3 = (f32[128,1024]{1,0:T(8,128)S(1)}, f32[128,1024]{1,0:T(8,128)S(1)}, u32[]{:S(2)}, u32[]{:S(2)}) collective-permute-start(f32[128,1024]{1,0:T(8,128)S(1)} %sums.8), channel_id=1, source_target_pairs={{0,128},{8,40},{16,144},{24,56},{32,160},{40,8},{48,176},{56,24},{... | collective-permute-start | bytes 1572872 | tf_op jit(solution)/shard_map/ppermute | solution.py:384
  94.8 13.1 %collective-permute-start.4 = (f32[128,1024]{1,0:T(8,128)S(1)}, f32[128,1024]{1,0:T(8,128)S(1)}, u32[]{:S(2)}, u32[]{:S(2)}) collective-permute-start(f32[128,1024]{1,0:T(8,128)S(1)} %get-tuple-element.27), channel_id=1, source_target_pairs={{0,64},{8,24},{16,80},{24,40},{32,96},{40,56},{48,112},{56,8},{64,... | collective-permute-start | bytes 1572872 | tf_op jit(solution)/shard_map/ppermute | solution.py:384
  96.2 6.1 %collective-permute-start.2 = (f32[128,1024]{1,0:T(8,128)S(1)}, f32[128,1024]{1,0:T(8,128)S(1)}, u32[]{:S(2)}, u32[]{:S(2)}) collective-permute-start(f32[128,1024]{1,0:T(8,128)S(1)} %sums.10), channel_id=1, source_target_pairs={{0,8},{8,0},{1,9},{9,1},{2,10},{10,2},{3,11},{11,3},{4,12},{12,4},... | collective-permute-start | bytes 1572872 | tf_op jit(solution)/shard_map/ppermute | solution.py:372
  96.8 11.0 %collective-permute-start.5 = (f32[128,1024]{1,0:T(8,128)S(1)}, f32[128,1024]{1,0:T(8,128)S(1)}, u32[]{:S(2)}, u32[]{:S(2)}) collective-permute-start(f32[128,1024]{1,0:T(8,128)S(1)} %get-tuple-element.30), channel_id=1, source_target_pairs={{0,192},{8,56},{16,208},{24,8},{32,224},{40,24},{48,240},{56,40},{... | collective-permute-start | bytes 1572872 | tf_op jit(solution)/shard_map/ppermute | solution.py:384
  108.0 5.4 %collective-permute-start.6 = (f32[32,1024]{1,0:T(8,128)S(1)}, f32[32,1024]{1,0:T(8,128)S(1)}, u32[]{:S(2)}, u32[]{:S(2)}) collective-permute-start(f32[32,1024]{1,0:T(8,128)S(1)} %get-tuple-element.32), channel_id=1, source_target_pairs={{0,32},{8,136},{16,48},{24,152},{32,0},{40,168},{48,16},{56,184},{... | collective-permute-start | bytes 393224 | tf_op jit(solution)/shard_map/ppermute | solution.py:384
  108.8 4.7 %collective-permute-start.7 = (f32[32,1024]{1,0:T(8,128)S(1)}, f32[32,1024]{1,0:T(8,128)S(1)}, u32[]{:S(2)}, u32[]{:S(2)}) collective-permute-start(f32[32,1024]{1,0:T(8,128)S(1)} %get-tuple-element.33), channel_id=1, source_target_pairs={{0,48},{8,200},{16,0},{24,216},{32,16},{40,232},{48,32},{56,248},{... | collective-permute-start | bytes 393224 | tf_op jit(solution)/shard_map/ppermute | solution.py:384
  110.5 5.0 %collective-permute-start.8 = (f32[32,1024]{1,0:T(8,128)S(1)}, f32[32,1024]{1,0:T(8,128)S(1)}, u32[]{:S(2)}, u32[]{:S(2)}) collective-permute-start(f32[32,1024]{1,0:T(8,128)S(1)} %get-tuple-element.34), channel_id=1, source_target_pairs={{0,16},{8,72},{16,32},{24,88},{32,48},{40,104},{48,0},{56,120},{64... | collective-permute-start | bytes 393224 | tf_op jit(solution)/shard_map/ppermute | solution.py:384
